TPU v7x, 32 devices: a whole 2x2x4 slice. The times are simulated.
32 devices in a mesh: grp: 2 (over core), dev: 16 (over z, y, x).
Axes of the slice: x: 2, y: 2, z: 4, core: 2. Of those that a mesh axis runs over, the one named last changes fastest.
Arguments:
- residual_in: bfloat16 [512, 2048], P(('grp', 'dev')), may hold values from -1.5 to 1.5
- queries: bfloat16 [2, 256, 4096], P(None, 'dev', 'grp'), may hold values from -2.5 to 2.5
- latest_key_value: bfloat16 [2, 256, 4, 256], P(None, 'dev', 'grp'), may hold values from -2.5 to 2.5
- key_value_cache: bfloat16 [2, 256, 4, 256, 256], P(None, 'dev', 'grp'), may hold values from -2.5 to 2.5
- cache_len: int32 [2, 256], P(None, 'dev'), may hold values from 1 to 256, 32768 in all within a row
- out_weight: bfloat16 [4096, 2048], P('grp'), may hold values from -0.09375 to 0.09375
- norm_gain: bfloat16 [2048], replicated, may hold values from 0.099609375 to 1.8984375
- router_weight: bfloat16 [2048, 32], replicated, may hold values from -0.125 to 0.125
- routes: int32 [512, 8], P(('grp', 'dev')), may hold values from 0 to 31, all different within a row; in each aligned block of 16 rows (0 to 15, 16 to 31, ...) at most 8 rows name the same one
- expert_gate_up: bfloat16 [32, 2048, 1536], P(('grp', 'dev')), may hold values from -0.125 to 0.125
- expert_down: bfloat16 [32, 768, 2048], P(('grp', 'dev')), may hold values from -0.21875 to 0.21875
Outputs:
- layer_out: bfloat16 [512, 2048], P(('grp', 'dev'))
Inputs may be any that keep to these rules, and one draw needn't show every extreme that they name: Each row of cache_len of 256 entries sums to 32768, and its largest entry is exactly 256. `routes`: the 8 experts of a row are distinct; in each aligned block of 16 rows (the rows of one device) no expert is named by more than 8 rows, a bound that some block reaches.
All inputs are finite; a program needn't handle non-finite values. No bound on the sum of `cache_len` on one device may be relied on, other than what follows from the above.
Results may differ from a plain program's by a relative error of at most 0.017.
Values may be sent and summed in bfloat16 or wider, within the bound.
A program may use at most 128 MiB of HBM per device.

v0:
```python
import math

import jax
import jax.numpy as jnp
from jax import lax
from jax.sharding import PartitionSpec as P

HEAD_SIZE = 128
FF = 768


def per_device(
    residual_in,
    queries,
    latest_key_value,
    key_value_cache,
    cache_len,
    out_weight,
    norm_gain,
    router_weight,
    routes,
    expert_gate_up,
    expert_down,
):
    halves = queries.shape[0]
    tokens = queries.shape[1]
    kv_heads = key_value_cache.shape[2]
    positions = key_value_cache.shape[3]
    q_heads = queries.shape[2] // HEAD_SIZE
    query_group = q_heads // kv_heads
    width = residual_in.shape[1]
    scale = 1.0 / math.sqrt(HEAD_SIZE)
    query_vector = queries.reshape(halves, tokens, kv_heads, query_group, HEAD_SIZE)
    scores = (
        jnp.einsum(
            "hrkgd,hrksd->hrkgs",
            query_vector,
            key_value_cache[..., :HEAD_SIZE],
            preferred_element_type=jnp.float32,
        )
        * scale
    )
    own_score = (
        jnp.einsum(
            "hrkgd,hrkd->hrkg",
            query_vector,
            latest_key_value[..., :HEAD_SIZE],
            preferred_element_type=jnp.float32,
        )
        * scale
    )
    visible = (
        jnp.arange(positions, dtype=jnp.int32)[None, None, None, None, :]
        < cache_len[:, :, None, None, None]
    )
    raised = jnp.where(visible, jnp.exp(scores), 0.0)
    own_raised = jnp.exp(own_score)
    totals = jnp.sum(raised, axis=-1) + own_raised
    weights = (raised / totals[..., None]).astype(jnp.bfloat16)
    own_weight = (own_raised / totals).astype(jnp.bfloat16)
    mixed = jnp.einsum(
        "hrkgs,hrksd->hrkgd",
        weights,
        key_value_cache[..., HEAD_SIZE:],
        preferred_element_type=jnp.float32,
    )
    mixed = (
        mixed
        + own_weight.astype(jnp.float32)[..., None]
        * latest_key_value[..., HEAD_SIZE:].astype(jnp.float32)[:, :, :, None, :]
    )
    attended = mixed.astype(jnp.bfloat16).reshape(halves * tokens, q_heads * HEAD_SIZE)
    partial_value = jnp.dot(attended, out_weight, preferred_element_type=jnp.float32).reshape(
        halves, tokens, width
    )
    summed = lax.psum(partial_value, "grp")
    projected = lax.dynamic_index_in_dim(summed, lax.axis_index("grp"), 0, keepdims=False)
    hidden = residual_in.astype(jnp.float32) + projected
    meansq = jnp.mean(hidden * hidden, axis=-1, keepdims=True)
    normed = (hidden * lax.rsqrt(meansq + 1e-06) * norm_gain.astype(jnp.float32)).astype(
        jnp.bfloat16
    )
    logits = jnp.dot(normed, router_weight, preferred_element_type=jnp.float32)
    picked = jnp.exp(jnp.take_along_axis(logits, routes, axis=1))
    gates = picked / jnp.sum(picked, axis=1, keepdims=True)
    batch_rows = routes.shape[0]
    topk = routes.shape[1]
    experts_all = router_weight.shape[1]
    capacity = max(2, 2 * batch_rows * topk // experts_all)
    flat_routes = routes.reshape(batch_rows * topk)
    onehot = (flat_routes[:, None] == jnp.arange(experts_all, dtype=jnp.int32)[None, :]).astype(
        jnp.int32
    )
    ranks = jnp.sum(onehot * (jnp.cumsum(onehot, axis=0) - 1), axis=1)
    target = flat_routes * capacity + ranks
    selector = (
        target[None, :] == jnp.arange(experts_all * capacity, dtype=jnp.int32)[:, None]
    ).astype(jnp.int32)
    selector = jnp.sum(selector.reshape(experts_all * capacity, batch_rows, topk), axis=2).astype(
        jnp.bfloat16
    )
    outgoing = jnp.dot(selector, normed, preferred_element_type=jnp.float32).astype(jnp.bfloat16)
    outgoing = outgoing.reshape(experts_all, capacity, width)
    received = lax.all_to_all(outgoing, ("grp", "dev"), split_axis=0, concat_axis=0, tiled=True)
    count = received.shape[0] * received.shape[1]
    gate_up = jnp.dot(
        received.reshape(count, width), expert_gate_up[0], preferred_element_type=jnp.float32
    )
    active = (jax.nn.silu(gate_up[:, :FF]) * gate_up[:, FF:]).astype(jnp.bfloat16)
    result = jnp.dot(active, expert_down[0], preferred_element_type=jnp.float32).astype(
        jnp.bfloat16
    )
    returned = lax.all_to_all(
        result.reshape(received.shape), ("grp", "dev"), split_axis=0, concat_axis=0, tiled=True
    )
    table = returned.reshape(experts_all * capacity, width)
    gathered = table[target].reshape(batch_rows, topk, width).astype(jnp.float32)
    combined = jnp.sum(gates[:, :, None] * gathered, axis=1)
    return (hidden + combined).astype(jnp.bfloat16)


def solution(mesh):
    placed = (
        P(("grp", "dev"), None),
        P(None, "dev", "grp"),
        P(None, "dev", "grp", None),
        P(None, "dev", "grp", None, None),
        P(None, "dev"),
        P("grp", None),
        P(),
        P(),
        P(("grp", "dev"), None),
        P(("grp", "dev"), None, None),
        P(("grp", "dev"), None, None),
    )
    return jax.shard_map(
        per_device, mesh=mesh, in_specs=placed, out_specs=P(("grp", "dev"), None), check_vma=False
    )
```

profile of v0, /device:TPU:0, one launch (start us, length us, event | category | flops | bytes accessed | tf_op | source)
XLA Modules:
  0.0 129.6 jit_solution(14752173730390621748)
XLA Ops:
  6.5 0.0 copy-start
  6.5 0.0 all-reduce.2.cloned.1.call-start
  6.5 0.9 iota_compare_fusion.2
  7.4 0.8 slice_convert_fusion
  8.3 0.9 copy.29
  9.2 0.2 fusion.39
  9.4 3.5 %fusion.48 = (f32[2,16,2,8]{3,2,1,0:T(2,128)S(1)}, f32[2,16,2,8,256]{4,3,2,1,0:T(8,128)S(1)}) fusion(bf16[2,16,2,8,128]{4,3,2,1,0:T(8,128)(2,1)S(1)} %bitcast.59, bf16[2,16,2,256,256]{4,3,2,1,0:T(8,128)(2,1)} %param.14, pred[2,16,256]{2,1,0:T(8,128)(4,1)S(1)} %iota_compare_fusion.2), kind=kOutput, calls=%fused_computation.61 | convolution fusion | flops 33947136 | bytes 4859904 | tf_op jit(solution)/shard_map/hrkgd,hrksd->hrkgs/dot_general | solution.py:35
  12.9 2.9 %fusion.29 = bf16[2,16,2,8,128]{4,3,2,1,0:T(8,128)(2,1)S(1)} fusion(bf16[2,16,2,256,256]{4,3,2,1,0:T(8,128)(2,1)} %param.14, f32[2,16,2,8,256]{4,3,2,1,0:T(8,128)S(1)} %get-tuple-element.12, f32[2,16,2,8]{3,2,1,0:T(2,128)S(1)} %get-tuple-element.6, f32[2,16,2,128]{3,2,1,0:T(2,128)S(1)} %get-tuple-element.7, f32[2,16,2,8]{3,2,1,0:T(2,128)S(1)} %get-tuple-element.5), kind=kOutput, calls=%fused_computation.20 | convolution fusion | flops 34013184 | bytes 4886528 | tf_op jit(solution)/shard_map/hrkgs,hrksd->hrkgd/dot_general | solution.py:61
  15.9 0.1 dot_general.29
  15.9 0.0 copy-start.4
  16.0 0.0 copy-start.5
  16.0 0.0 copy-start.2
  16.0 5.7 %fusion = f32[2,16,2048]{2,1,0:T(8,128)} fusion(bf16[2,16,2048]{2,1,0:T(8,128)(2,1)S(1)} %dot_general.29, bf16[2048,2048]{1,0:T(8,128)(2,1)} %param.16), kind=kOutput, calls=%fused_computation.2 | convolution fusion | flops 268435456 | bytes 8781824 | tf_op jit(solution)/shard_map/dot_general | solution.py:73
  21.6 0.0 all-reduce.2.cloned.1.call-update
  21.7 0.0 copy-done.4
  21.7 0.1 copy.25
  21.7 0.1 eq.29
  21.8 0.0 copy-done.5
  21.9 0.1 fusion.38
  21.9 0.2 reduce_window_sum.11
  22.1 0.2 select_reduce_fusion
  22.3 0.1 reduce_sum.62
  22.4 0.1 convert_reduce_fusion
  22.5 20.3 %all-reduce.2.cloned.1.call-done = f32[2,16,2048]{2,1,0:T(8,128)} async-done(((f32[2,16,2048]{2,1,0:T(8,128)}), f32[2,16,2048]{2,1,0:T(8,128)}) %all-reduce.2.cloned.1.call-update) | async-done | bytes 262160 | tf_op jit(solution)/shard_map/psum | solution.py:76
  42.8 0.0 copy-done.2
  42.8 1.0 multiply_reduce_fusion
  43.8 1.0 multiply_convert_fusion
  44.8 0.5 fusion.13
  45.3 33.6 %all_to_all.10 = bf16[32,8,2048]{2,1,0:T(8,128)(2,1)S(1)} all-to-all(bf16[32,8,2048]{2,1,0:T(8,128)(2,1)S(1)} %fusion.13), channel_id=1, replica_groups=mesh['grp'=2,'dev'=16] {'grp','dev'}, dimensions={0} | all-to-all | bytes 2097152 | tf_op jit(solution)/shard_map/all_to_all | solution.py:104
  78.9 4.6 %fusion.2 = f32[256,1536]{1,0:T(8,128)S(1)} fusion(bf16[1,2048,1536]{2,1,0:T(8,128)(2,1)} %param.20, bf16[32,8,2048]{2,1,0:T(8,128)(2,1)S(1)} %all_to_all.10), kind=kOutput, calls=%fused_computation.4 | convolution fusion | flops 1610612736 | bytes 8912896 | tf_op jit(solution)/shard_map/dot_general | solution.py:106
  83.5 0.0 copy-done
  83.5 0.0 copy-start.3
  83.5 2.1 %fusion.14 = bf16[32,8,2048]{2,1,0:T(8,128)(2,1)} fusion(bf16[1,768,2048]{2,1,0:T(8,128)(2,1)S(1)} %copy-done, f32[256,1536]{1,0:T(8,128)S(1)} %fusion.2), kind=kOutput, calls=%fused_computation.15 | convolution fusion | flops 807010304 | bytes 5767168 | tf_op jit(solution)/shard_map/dot_general | solution.py:110
  85.6 3.4 %all-to-all-start.1 = ((bf16[32,8,2048]{2,1,0:T(8,128)(2,1)}), bf16[32,8,2048]{2,1,0:T(8,128)(2,1)}, u32[]{:S(2)}, u32[]{:S(2)}) async-start(bf16[32,8,2048]{2,1,0:T(8,128)(2,1)} %fusion.14), calls=%async_computation.1 | async-start | bytes 2097152 | tf_op jit(solution)/shard_map/all_to_all | solution.py:113
  89.0 0.1 copy.22
  89.1 0.1 reshape.125
  89.2 0.1 mul.100
  89.3 0.0 copy-done.3
  89.3 0.1 fusion.49
  89.4 1.3 gather_fusion.1
  90.7 0.0 copy-start.1
  90.7 0.1 reshape.128
  90.8 0.1 copy.23
  90.9 0.1 copy.24
  91.0 26.0 %all-to-all-done.1 = bf16[32,8,2048]{2,1,0:T(8,128)(2,1)} async-done(((bf16[32,8,2048]{2,1,0:T(8,128)(2,1)}), bf16[32,8,2048]{2,1,0:T(8,128)(2,1)}, u32[]{:S(2)}, u32[]{:S(2)}) %all-to-all-start.1) | async-done | bytes 1048608 | tf_op jit(solution)/shard_map/all_to_all | solution.py:113
  117.0 3.6 %gather_fusion = bf16[128,2048]{1,0:T(8,128)(2,1)} fusion(bf16[256,2048]{1,0:T(8,128)(2,1)} %bitcast.11, s32[1024]{0:T(1024)S(1)} %pad_clamp_fusion), kind=kCustom, calls=%fused_computation | custom fusion | bytes 1049088 | tf_op jit(solution)/shard_map/gather | solution.py:117
  120.6 1.5 %fusion.32 = f32[16,2048]{1,0:T(8,128)S(1)} fusion(bf16[128,2048]{1,0:T(8,128)(2,1)} %gather_fusion, f32[16,8]{1,0:T(8,128)S(1)} %copy.24), kind=kLoop, calls=%fused_computation.22 | loop fusion | flops 753664 | bytes 655872 | tf_op jit(solution)/shard_map/reduce_sum | solution.py:118
  122.1 0.7 add_convert_fusion
  (10 shorter events, 0.1 us)
Async XLA Ops:
  6.5 77.0 %copy-start = (bf16[1,768,2048]{2,1,0:T(8,128)(2,1)S(1)}, bf16[1,768,2048]{2,1,0:T(8,128)(2,1)}, u32[]{:S(2)}) copy-start(bf16[1,768,2048]{2,1,0:T(8,128)(2,1)} %param.21) | copy-start | bytes 9437188
  6.5 36.2 %all-reduce.2.cloned.1.call-start = ((), (), s32[]{:S(2)}) async-start(), calls=%async_computation.2 | async-start | bytes 524288 | tf_op jit(solution)/shard_map/psum | solution.py:76
  15.9 5.7 %copy-start.4 = (s32[16,8]{0,1:T(8,128)S(1)}, s32[16,8]{0,1:T(8,128)}, u32[]{:S(2)}) copy-start(s32[16,8]{0,1:T(8,128)} %param.19) | copy-start | bytes 1540
  16.0 5.9 %copy-start.5 = (bf16[2048]{0:T(1024)(128)(2,1)S(1)}, bf16[2048]{0:T(1024)(128)(2,1)}, u32[]{:S(2)}) copy-start(bf16[2048]{0:T(1024)(128)(2,1)} %param.17) | copy-start | bytes 12292
  16.0 26.8 %copy-start.2 = (bf16[16,2048]{1,0:T(8,128)(2,1)S(1)}, bf16[16,2048]{1,0:T(8,128)(2,1)}, u32[]{:S(2)}) copy-start(bf16[16,2048]{1,0:T(8,128)(2,1)} %param.11) | copy-start | bytes 196612
  83.5 5.8 %copy-start.3 = (bf16[2048,32]{0,1:T(8,128)(2,1)S(1)}, bf16[2048,32]{0,1:T(8,128)(2,1)}, u32[]{:S(2)}) copy-start(bf16[2048,32]{0,1:T(8,128)(2,1)} %param.18) | copy-start | bytes 393220
  85.6 31.4 %all-to-all-start.1 = ((bf16[32,8,2048]{2,1,0:T(8,128)(2,1)}), bf16[32,8,2048]{2,1,0:T(8,128)(2,1)}, u32[]{:S(2)}, u32[]{:S(2)}) async-start(bf16[32,8,2048]{2,1,0:T(8,128)(2,1)} %fusion.14), calls=%async_computation.1 | async-start | bytes 2097152 | tf_op jit(solution)/shard_map/all_to_all | solution.py:113
  90.7 31.4 %copy-start.1 = (f32[2,16,2048]{2,1,0:T(8,128)S(1)}, f32[2,16,2048]{2,1,0:T(8,128)}, u32[]{:S(2)}) copy-start(f32[2,16,2048]{2,1,0:T(8,128)} %all-reduce.2.cloned.1.call-done) | copy-start | bytes 786436
Sparse Core Ops, SparseCore 0:
  21.8 20.9 all-reduce.1
where the time goes:
time: 130 us
  waiting for transfers between devices  46.3 us (36%)
  blocking collectives  33.6 us (26%)
  matrix products  19.5 us (15%)
  between operations  13.6 us (10%)
  local copies, waits for them, and re-layouts  6.64 us (5%)
  other arithmetic  6.56 us (5%)
  starting transfers between devices  3.38 us (3%)
    all_to_all x1, blocking collectives, per_device(): lax.all_to_all(outgoing, ('grp', 'dev'), split_axis=0, concat_axis=0, til...  33.6 us
    all_to_all x1, waiting for transfers between devices, per_device(): lax.all_to_all(result.reshape(received.shape), ('grp', 'dev'), split_axis...  26 us
    psum x1, waiting for transfers between devices, per_device(): summed = lax.psum(partial_value, 'grp')  20.3 us
    dot_general x1, matrix products, per_device(): jnp.dot(attended, out_weight, preferred_element_type=jnp.float32)  5.66 us
    dot_general x1, matrix products, per_device(): jnp.dot(received.reshape(count, width), expert_gate_up[0], preferred_elem...  4.56 us
    gather x1, local copies, waits for them, and re-layouts, per_device(): table[target].reshape(batch_rows, topk, width).astype(jnp.float32)  3.62 us
    dot_general x1, matrix products, per_device(): jnp.einsum('hrkgd,hrksd->hrkgs', query_vector, key_value_cache[..., :HEAD...  3.5 us
    all_to_all x1, starting transfers between devices, per_device(): lax.all_to_all(result.reshape(received.shape), ('grp', 'dev'), split_axis...  3.37 us
  transfers between devices with their start and end apart: 2, of which 2 were waited for; matrix products, arithmetic and copies ran while one was open for 2% of the time, Pallas kernels for 0%

commit v1 on v0

v1 whole, which is shorter than its diff:
```python
import functools
import math

import jax
import jax.numpy as jnp
from jax import lax
from jax.experimental import pallas as pl
from jax.experimental.pallas import tpu as pltpu
from jax.sharding import PartitionSpec as P

HEAD_SIZE = 128
MESH = pl.DeviceIdType.MESH
ROWS_STEP = 8
VMEM_LIMIT = 56 * 1024 * 1024


def attend_kernel(steps, lens_ref, q_ref, new_ref, cache_ref, wo_hbm, out_ref, att, wo, sem):
    i = pl.program_id(0)
    rows, kv_heads, positions, _ = cache_ref.shape
    q_heads = q_ref.shape[1] // HEAD_SIZE
    group = q_heads // kv_heads
    scale = 1.0 / math.sqrt(HEAD_SIZE)

    @pl.when(i == 0)
    def _():
        pltpu.make_async_copy(wo_hbm, wo, sem).start()

    q = q_ref[...].astype(jnp.float32)
    q = jnp.stack([q[:, j * HEAD_SIZE : (j + 1) * HEAD_SIZE] for j in range(q_heads)], axis=0)
    q = jnp.swapaxes(q, 0, 1)
    new = new_ref[...].astype(jnp.float32)
    place = lax.broadcasted_iota(jnp.int32, (group, positions), 1)
    mixed = []
    for r in range(rows):
        length = lens_ref[i * rows + r]
        heads = []
        for h in range(kv_heads):
            qh = q[r, h * group : (h + 1) * group]
            s = lax.dot_general(
                qh.astype(jnp.bfloat16),
                cache_ref[r, h, :, :HEAD_SIZE],
                (((1,), (1,)), ((), ())),
                preferred_element_type=jnp.float32,
            )
            e = jnp.where(place < length, jnp.exp(s * scale), 0.0)
            fresh = new[r, h : h + 1]
            own = jnp.exp(jnp.sum(qh * fresh[:, :HEAD_SIZE], axis=1, keepdims=True) * scale)
            total = jnp.sum(e, axis=1, keepdims=True) + own
            w = (e / total).astype(jnp.bfloat16)
            own_w = (own / total).astype(jnp.bfloat16).astype(jnp.float32)
            o = jnp.dot(w, cache_ref[r, h, :, HEAD_SIZE:], preferred_element_type=jnp.float32)
            heads.append(o + own_w * fresh[:, HEAD_SIZE:])
        mixed.append(jnp.concatenate(heads, axis=0))
    mixed = jnp.swapaxes(jnp.stack(mixed, axis=0), 0, 1)
    att[i] = jnp.concatenate([mixed[j] for j in range(q_heads)], axis=1)

    @pl.when(i == steps - 1)
    def _():
        pltpu.make_async_copy(wo_hbm, wo, sem).wait()
        a = att[...].reshape(steps * rows, q_heads * HEAD_SIZE).astype(jnp.bfloat16)
        out_ref[...] = jnp.dot(a, wo[...], preferred_element_type=jnp.float32)


def attend(queries, latest, cache, lens, out_weight):
    total, q_width = queries.shape
    kv_heads, positions, kv_width = cache.shape[1:]
    width = out_weight.shape[1]
    steps = total // ROWS_STEP
    return pl.pallas_call(
        functools.partial(attend_kernel, steps),
        grid=(steps,),
        out_shape=jax.ShapeDtypeStruct((total, width), jnp.float32),
        in_specs=[
            pl.BlockSpec(memory_space=pltpu.SMEM),
            pl.BlockSpec((ROWS_STEP, q_width), lambda i: (i, 0)),
            pl.BlockSpec((ROWS_STEP, kv_heads, kv_width), lambda i: (i, 0, 0)),
            pl.BlockSpec((ROWS_STEP, kv_heads, positions, kv_width), lambda i: (i, 0, 0, 0)),
            pl.BlockSpec(memory_space=pl.ANY),
        ],
        out_specs=pl.BlockSpec((total, width), lambda i: (0, 0)),
        scratch_shapes=[
            pltpu.VMEM((steps, ROWS_STEP, q_width), jnp.float32),
            pltpu.VMEM(out_weight.shape, out_weight.dtype),
            pltpu.SemaphoreType.DMA,
        ],
        compiler_params=pltpu.CompilerParams(vmem_limit_bytes=VMEM_LIMIT),
        name="attend",
    )(lens, queries, latest, cache, out_weight)


def moe_kernel(
    n,
    bits,
    partial_ref,
    res_ref,
    gain_ref,
    router_ref,
    routes_ref,
    wgu_hbm,
    wd_hbm,
    out_ref,
    wgu,
    wd,
    xsib,
    hid,
    gath,
    act,
    part,
    rsib,
    racc,
    wsem,
    xsem,
    gsend,
    grecv,
    ssend,
    srecv,
    bsend,
    brecv,
    rsend,
    rrecv,
):
    g = lax.axis_index("grp")
    d = lax.axis_index("dev")
    tok, width = res_ref.shape
    experts = router_ref.shape[1]
    ff = wd.shape[0]
    sib = (1 - g, d)

    def peer(j):
        m = 1 << (bits - 1 - j)
        if bits >= 2 and j == bits - 2:
            m = 1 + g
        elif bits >= 2 and j == bits - 1:
            m = 2 - g
        return (g, d + m * (1 - 2 * ((d // m) % 2)))

    peers = [peer(j) for j in range(bits)]
    load_gu = pltpu.make_async_copy(wgu_hbm.at[0], wgu, wsem.at[0])
    load_d = pltpu.make_async_copy(wd_hbm.at[0], wd, wsem.at[1])
    load_gu.start()
    load_d.start()

    barrier = pltpu.get_barrier_semaphore()
    for target in peers + [sib]:
        pl.semaphore_signal(barrier, inc=1, device_id=target, device_id_type=MESH)
    pl.semaphore_wait(barrier, bits + 1)

    def remote(src, dst, send, recv, target):
        return pltpu.make_async_remote_copy(
            src_ref=src,
            dst_ref=dst,
            send_sem=send,
            recv_sem=recv,
            device_id=target,
            device_id_type=MESH,
        )

    swap = remote(partial_ref.at[1 - g], xsib, xsem.at[0], xsem.at[1], sib)
    swap.start()
    swap.wait()
    hidden = res_ref[...].astype(jnp.float32) + (partial_ref[g] + xsib[...])
    hid[...] = hidden
    meansq = jnp.mean(hidden * hidden, axis=-1, keepdims=True)
    normed = (hidden * lax.rsqrt(meansq + 1e-06) * gain_ref[...].astype(jnp.float32)).astype(
        jnp.bfloat16
    )
    logits = jnp.dot(normed, router_ref[...], preferred_element_type=jnp.float32)
    lane = lax.broadcasted_iota(jnp.int32, (tok, experts), 1)
    routes = routes_ref[...]
    routed = lane == routes[:, 0:1]
    for k in range(1, routes.shape[1]):
        routed = jnp.logical_or(routed, lane == routes[:, k : k + 1])
    picked = jnp.where(routed, jnp.exp(logits), 0.0)
    gates = picked / jnp.sum(picked, axis=1, keepdims=True)
    extra = gath.shape[3] - width
    if extra > experts:
        gates = jnp.concatenate([gates, jnp.zeros((tok, extra - experts), jnp.float32)], axis=1)
    gath[0, 0, :, :width] = normed
    gath[0, 0, :, width:] = gates.astype(jnp.bfloat16)

    sends = []

    def forward(slot):
        first = slot.bit_length()
        for j in range(bits - 1, first - 1, -1):
            there = slot | (1 << j)
            sends.append(
                remote(gath.at[0, slot], gath.at[0, there], gsend.at[there], grecv.at[there], peers[j])
            )
            sends[-1].start()
        sends.append(remote(gath.at[0, slot], gath.at[1, slot], ssend.at[slot], srecv.at[slot], sib))
        sends[-1].start()

    def arrived(slot):
        remote(gath.at[0, slot], gath.at[0, slot], gsend.at[slot], grecv.at[slot], sib).wait_recv()

    def arrived_sib(slot):
        remote(gath.at[0, slot], gath.at[1, slot], ssend.at[slot], srecv.at[slot], sib).wait_recv()

    half = n // 2
    forward(0)
    for slot in range(1, half):
        arrived(slot)
        forward(slot)

    expert = g * n + d
    group = min(8, half)
    rows = 2 * group * tok

    def gate_up(base, t, tile):
        x = gath[:, pl.ds(base, group), :, :width].reshape(rows, width)
        gate = jnp.dot(x, wgu[:, t : t + tile], preferred_element_type=jnp.float32)
        up = jnp.dot(x, wgu[:, ff + t : ff + t + tile], preferred_element_type=jnp.float32)
        act[:, t : t + tile] = (gate / (1.0 + jnp.exp(-gate)) * up).astype(jnp.bfloat16)

    def down(base):
        weights = gath[:, pl.ds(base, group), :, width:].reshape(rows, extra).astype(jnp.float32)
        mine = lax.broadcasted_iota(jnp.int32, (rows, extra), 1) == expert
        weight = jnp.sum(jnp.where(mine, weights, 0.0), axis=1, keepdims=True)
        tile = 512
        for t in range(0, width, tile):
            y = jnp.dot(act[...], wd[:, t : t + tile], preferred_element_type=jnp.float32)
            y = (y * weight).astype(jnp.bfloat16).reshape(2, group, tok, tile)
            part[:, pl.ds(base, group), :, t : t + tile] = y

    FT = 256
    for slot in range(half):
        arrived_sib(slot)
    load_gu.wait()
    pending = list(range(half, n))
    tiles = list(range(0, ff, FT))
    for at in range(0, half, group):
        for t in tiles:
            gate_up(at, t, FT)
            if at == 0:
                count = -(-half // len(tiles))
                for slot in pending[:count]:
                    arrived(slot)
                    forward(slot)
                pending = pending[count:]
        if at == 0:
            load_d.wait()
        down(at)

    def give(slot):
        sends.append(remote(part.at[1, slot], rsib.at[slot], bsend.at[slot], brecv.at[slot], sib))
        sends[-1].start()

    def taken(slot):
        remote(part.at[1, slot], rsib.at[slot], bsend.at[slot], brecv.at[slot], sib).wait_recv()
        part[0, slot] = (
            part[0, slot].astype(jnp.float32) + rsib[slot].astype(jnp.float32)
        ).astype(jnp.bfloat16)

    order = [bits - 2, bits - 1] + list(range(bits - 3, -1, -1)) if bits >= 2 else [0]

    def ship(slot, step):
        j = order[step]
        there = slot ^ (1 << j)
        sends.append(
            remote(part.at[0, slot], racc.at[slot], rsend.at[slot], rrecv.at[slot], peers[j])
        )
        sends[-1].start()

    def absorb(slot, step):
        j = order[step]
        source = slot | (1 << j)
        remote(part.at[0, slot], racc.at[source], rsend.at[source], rrecv.at[source], sib).wait_recv()
        part[0, slot] = (
            part[0, slot].astype(jnp.float32) + racc[source].astype(jnp.float32)
        ).astype(jnp.bfloat16)

    for slot in range(half):
        give(slot)
    for slot in range(half, n):
        arrived_sib(slot)
    for at in range(half, n, group):
        for t in tiles:
            gate_up(at, t, FT)
            if at == half and t == tiles[0]:
                for slot in range(half):
                    taken(slot)
                    if slot & (1 << order[0]):
                        ship(slot, 0)
        down(at)
    for slot in range(half, n):
        give(slot)
    for slot in reversed(range(half, n)):
        taken(slot)
        if slot & (1 << order[0]):
            ship(slot, 0)

    live = [s for s in range(n) if not s & (1 << order[0])]
    for step in range(1, len(order)):
        j = order[step]
        out_going = [s for s in live if s & (1 << j)]
        staying = [s for s in live if not s & (1 << j)]
        for s in out_going:
            absorb(s, step - 1)
            ship(s, step)
        for s in staying:
            absorb(s, step - 1)
        live = staying
    source = 1 << order[-1]
    remote(part.at[0, 0], racc.at[source], rsend.at[source], rrecv.at[source], sib).wait_recv()
    out_ref[...] = (
        hid[...] + (part[0, 0].astype(jnp.float32) + racc[source].astype(jnp.float32))
    ).astype(jnp.bfloat16)
    for copy in sends:
        copy.wait_send()


def moe(n, partial, residual, gain, router, routes, gate_up, down):
    tok, width = residual.shape
    bits = n.bit_length() - 1
    extra = -(-router.shape[1] // 128) * 128
    group = min(8, n // 2)
    bf16 = jnp.bfloat16
    dma = pltpu.SemaphoreType.DMA
    vmem = pl.BlockSpec(memory_space=pltpu.VMEM)
    hbm = pl.BlockSpec(memory_space=pl.ANY)
    return pl.pallas_call(
        functools.partial(moe_kernel, n, bits),
        out_shape=jax.ShapeDtypeStruct((tok, width), bf16),
        in_specs=[vmem] * 5 + [hbm] * 2,
        out_specs=vmem,
        scratch_shapes=[
            pltpu.VMEM(gate_up.shape[1:], bf16),
            pltpu.VMEM(down.shape[1:], bf16),
            pltpu.VMEM((tok, width), jnp.float32),
            pltpu.VMEM((tok, width), jnp.float32),
            pltpu.VMEM((2, n, tok, width + extra), bf16),
            pltpu.VMEM((2 * group * tok, down.shape[1]), bf16),
            pltpu.VMEM((2, n, tok, width), bf16),
            pltpu.VMEM((n, tok, width), bf16),
            pltpu.VMEM((n, tok, width), bf16),
            dma((2,)),
            dma((2,)),
            dma((n,)),
            dma((n,)),
            dma((n,)),
            dma((n,)),
            dma((n,)),
            dma((n,)),
            dma((n,)),
            dma((n,)),
        ],
        compiler_params=pltpu.CompilerParams(
            collective_id=0, has_side_effects=True, vmem_limit_bytes=VMEM_LIMIT
        ),
        name="moe",
    )(partial, residual, gain, router, routes, gate_up, down)


def solution(mesh):
    n = mesh.shape["dev"]

    def per_device(
        residual_in,
        queries,
        latest_key_value,
        key_value_cache,
        cache_len,
        out_weight,
        norm_gain,
        router_weight,
        routes,
        expert_gate_up,
        expert_down,
    ):
        halves, tokens = queries.shape[:2]
        total = halves * tokens
        partial = attend(
            queries.reshape(total, -1),
            latest_key_value.reshape((total,) + latest_key_value.shape[2:]),
            key_value_cache.reshape((total,) + key_value_cache.shape[2:]),
            cache_len.reshape(total),
            out_weight,
        )
        return moe(
            n,
            partial.reshape(halves, tokens, -1),
            residual_in,
            norm_gain.reshape(1, -1),
            router_weight,
            routes,
            expert_gate_up,
            expert_down,
        )

    placed = (
        P(("grp", "dev"), None),
        P(None, "dev", "grp"),
        P(None, "dev", "grp", None),
        P(None, "dev", "grp", None, None),
        P(None, "dev"),
        P("grp", None),
        P(),
        P(),
        P(("grp", "dev"), None),
        P(("grp", "dev"), None, None),
        P(("grp", "dev"), None, None),
    )
    return jax.shard_map(
        per_device, mesh=mesh, in_specs=placed, out_specs=P(("grp", "dev"), None), check_vma=False
    )
```

time: 130 us -> 75.8 us (0.58)
  Pallas kernels: 0 us -> 69.2 us
  waiting for transfers between devices: 46.3 us -> 0 us
  blocking collectives: 33.6 us -> 0 us
  matrix products: 19.5 us -> 0 us
  between operations: 13.6 us -> 0.03 us
  other arithmetic: 6.56 us -> 0 us
  starting transfers between devices: 3.38 us -> 0 us
    pallas_call x0 -> x2, Pallas kernels: none -> 69.2 us  [the longest x1 49.3 us: moe(): pl.pallas_call(functools.partial(moe_kernel, n, bits), out_shape=jax.Shap...]
    all_to_all x1 -> x0, blocking collectives: 33.6 us -> none  [per_device(): lax.all_to_all(outgoing, ('grp', 'dev'), split_axis=0, concat_axis=0, til...]
    all_to_all x1 -> x0, waiting for transfers between devices: 26 us -> none  [per_device(): lax.all_to_all(result.reshape(received.shape), ('grp', 'dev'), split_axis...]
    psum x1 -> x0, waiting for transfers between devices: 20.3 us -> none  [per_device(): summed = lax.psum(partial_value, 'grp')]
    dot_general x8 -> x0, matrix products: 19.5 us -> none  [the longest x1 5.66 us: per_device(): jnp.dot(attended, out_weight, preferred_element_type=jnp.float32)]
    gather x6 -> x0, local copies, waits for them, and re-layouts: 5.21 us -> none  [the longest x1 3.62 us: per_device(): table[target].reshape(batch_rows, topk, width).astype(jnp.float32)]
    all_to_all x1 -> x0, starting transfers between devices: 3.37 us -> none  [per_device(): lax.all_to_all(result.reshape(received.shape), ('grp', 'dev'), split_axis...]
    reduce_sum x5 -> x0, other arithmetic: 2.84 us -> none  [the longest x1 1.49 us: per_device(): combined = jnp.sum(gates[:, :, None] * gathered, axis=1)]
  transfers between devices with their start and end apart: 2 -> 0, of which waited for: 2 -> 0; matrix products, arithmetic and copies ran while one was open for 2% -> 0% of each run, Pallas kernels for 0% -> 0%
where the time goes in v1:
time: 75.8 us; the launch traced here: 75.6 us
  Pallas kernels  69.2 us (91%)
  local copies, waits for them, and re-layouts  6.35 us (8%)
    pallas_call x1, Pallas kernels, moe(): pl.pallas_call(functools.partial(moe_kernel, n, bits), out_shape=jax.Shap...  49.3 us
    pallas_call x1, Pallas kernels, attend(): pl.pallas_call(functools.partial(attend_kernel, steps), grid=(steps,), ou...  19.9 us
    unnamed x5, local copies, waits for them, and re-layouts  3.82 us

profile of v1, /device:TPU:0, one launch (start us, length us, event | category | flops | bytes accessed | tf_op | source)
XLA Modules:
  0.0 75.6 jit_solution(13158025122845539859)
XLA Ops:
  0.0 1.2 %reshape.18.lens_ref = s32[32]{0:T(128)} reshape(s32[2,16]{1,0:T(2,128)} %param.15) | data formatting | bytes 256 | tf_op jit(solution)/shard_map/reshape | solution.py:377
  1.2 1.3 %reshape.23.gain_ref = bf16[1,2048]{1,0:T(2,128)(2,1)} reshape(bf16[2048]{0:T(1024)(128)(2,1)} %param.17) | data formatting | bytes 8192 | tf_op jit(solution)/shard_map/reshape | solution.py:384
  2.5 1.4 %copy.13.routes_ref = s32[16,8]{1,0:T(8,128)} copy(s32[16,8]{0,1:T(8,128)} %param.19) | data formatting | bytes 1024 | tf_op args[8]
  3.9 0.0 copy-start
  3.9 19.9 %attend.1 = f32[32,2048]{1,0:T(8,128)} custom-call(s32[32]{0:T(128)} %reshape.18.lens_ref, bf16[32,2048]{1,0:T(8,128)(2,1)} %bitcast.6, bf16[32,2,256]{2,1,0:T(2,128)(2,1)} %bitcast.7, bf16[32,2,256,256]{3,2,1,0:T(8,128)(2,1)} %bitcast.4, bf16[2048,2048]{1,0:T(8,128)(2,1)} %wo_hbm.1), custom_call_target="tpu_custom_call" | custom-call | tf_op jit(solution)/shard_map/attend/pallas_call | solution.py:69
  23.8 0.0 copy-done
  23.8 1.0 %copy.12.router_ref = bf16[2048,32]{1,0:T(8,128)(2,1)} copy(bf16[2048,32]{0,1:T(8,128)(2,1)S(1)} %copy-done) | data formatting | bytes 262144 | tf_op args[7]
  24.8 49.3 %moe.1 = bf16[16,2048]{1,0:T(8,128)(2,1)} custom-call(f32[2,16,2048]{2,1,0:T(8,128)} %bitcast.5, bf16[16,2048]{1,0:T(8,128)(2,1)} %res_ref.1, bf16[1,2048]{1,0:T(2,128)(2,1)} %reshape.23.gain_ref, bf16[2048,32]{1,0:T(8,128)(2,1)} %copy.12.router_ref, s32[16,8]{1,0:T(8,128)} %copy.13.routes_ref, bf16[1,2048,1536]{2,1,0:T(8,128)(2,1)} %wgu_hbm.1, ...), custom_call_target="tpu_custom_call" | custom-call | tf_op jit(solution)/shard_map/moe/pallas_call | solution.py:322
  74.1 1.5 %copy.15 = bf16[16,2048]{1,0:T(8,128)(2,1)} copy(bf16[16,2048]{1,0:T(8,128)(2,1)} %moe.1) | data formatting | bytes 131072
Async XLA Ops:
  3.9 19.9 %copy-start = (bf16[2048,32]{0,1:T(8,128)(2,1)S(1)}, bf16[2048,32]{0,1:T(8,128)(2,1)}, u32[]{:S(2)}) copy-start(bf16[2048,32]{0,1:T(8,128)(2,1)} %param.18) | copy-start | bytes 393220

commit v2 on v1

v2 whole, which is shorter than its diff:
```python
import functools
import math

import jax
import jax.numpy as jnp
from jax import lax
from jax.experimental import pallas as pl
from jax.experimental.pallas import tpu as pltpu
from jax.sharding import PartitionSpec as P

HEAD_SIZE = 128
MESH = pl.DeviceIdType.MESH
ROWS_STEP = 8
OUT_TILE = 512
VMEM_LIMIT = 60 * 1024 * 1024


def layer_kernel(
    n,
    bits,
    lens_ref,
    q_ref,
    new_ref,
    cache_hbm,
    wo_hbm,
    res_ref,
    gain_ref,
    router_ref,
    routes_ref,
    wgu_hbm,
    wd_hbm,
    out_ref,
    kv,
    wo,
    wgu,
    wd,
    qs,
    att,
    pout,
    xsib,
    hid,
    gath,
    act,
    part,
    rsib,
    racc,
    ksem,
    wsem,
    xsend,
    xrecv,
    gsend,
    grecv,
    ssend,
    srecv,
    bsend,
    brecv,
    rsend,
    rrecv,
):
    g = lax.axis_index("grp")
    d = lax.axis_index("dev")
    tok, width = res_ref.shape
    experts = router_ref.shape[0]
    ff = wd.shape[0]
    sib = (1 - g, d)
    halves, tokens = q_ref.shape[:2]
    per_half = tokens // ROWS_STEP
    steps = halves * per_half
    kv_heads, positions = cache_hbm.shape[2:4]
    q_heads = q_ref.shape[2] // HEAD_SIZE
    group = q_heads // kv_heads
    scale = 1.0 / math.sqrt(HEAD_SIZE)

    def load_kv(half, s):
        return pltpu.make_async_copy(
            cache_hbm.at[half, pl.ds(s * ROWS_STEP, ROWS_STEP)],
            kv.at[half, s],
            ksem.at[half, s],
        )

    load_o = pltpu.make_async_copy(wo_hbm, wo, wsem.at[0])
    load_gu = pltpu.make_async_copy(wgu_hbm.at[0], wgu, wsem.at[1])
    load_d = pltpu.make_async_copy(wd_hbm.at[0], wd, wsem.at[2])
    for half in range(halves):
        for s in range(per_half):
            load_kv(half, s).start()

    def peer(j):
        m = 1 << (bits - 1 - j)
        if bits >= 2 and j == bits - 2:
            m = 1 + g
        elif bits >= 2 and j == bits - 1:
            m = 2 - g
        return (g, d + m * (1 - 2 * ((d // m) % 2)))

    peers = [peer(j) for j in range(bits)]
    barrier = pltpu.get_barrier_semaphore()
    for target in peers + [sib]:
        pl.semaphore_signal(barrier, inc=1, device_id=target, device_id_type=MESH)

    def remote(src, dst, send, recv, target):
        return pltpu.make_async_remote_copy(
            src_ref=src,
            dst_ref=dst,
            send_sem=send,
            recv_sem=recv,
            device_id=target,
            device_id_type=MESH,
        )

    for half in range(halves):
        q = q_ref[half].astype(jnp.float32)
        q = jnp.stack([q[:, j * HEAD_SIZE : (j + 1) * HEAD_SIZE] for j in range(q_heads)], axis=0)
        qs[half] = jnp.swapaxes(q, 0, 1)

    pairs = [(r, h) for r in range(ROWS_STEP) for h in range(kv_heads)]

    def attend(i, carry):
        half = i // per_half
        s = i % per_half
        load_kv(half, s).wait()

        @pl.when(i == 0)
        def _():
            load_o.start()

        first = pl.multiple_of(s * ROWS_STEP, ROWS_STEP)
        q = qs[half, pl.ds(first, ROWS_STEP)].reshape(ROWS_STEP, kv_heads, group, HEAD_SIZE)
        new = new_ref[half, pl.ds(first, ROWS_STEP)].astype(jnp.float32)[:, :, None, :]
        own = jnp.exp(jnp.sum(q * new[..., :HEAD_SIZE], axis=-1, keepdims=True) * scale)
        qb = q.astype(jnp.bfloat16)
        place = lax.broadcasted_iota(jnp.int32, (group, positions), 1)
        lens = [lens_ref[half, first + r] for r in range(ROWS_STEP)]
        scores = [
            lax.dot_general(
                qb[r, h],
                kv[half, s, r, h, :, :HEAD_SIZE],
                (((1,), (1,)), ((), ())),
                preferred_element_type=jnp.float32,
            )
            for r, h in pairs
        ]
        raised = [
            jnp.where(place < lens[r], jnp.exp(x * scale), 0.0) for (r, h), x in zip(pairs, scores)
        ]
        inverse = [
            1.0 / (jnp.sum(e, axis=1, keepdims=True) + own[r, h]) for (r, h), e in zip(pairs, raised)
        ]
        weights = [(e * v).astype(jnp.bfloat16) for e, v in zip(raised, inverse)]
        mixed = [
            jnp.dot(w, kv[half, s, r, h, :, HEAD_SIZE:], preferred_element_type=jnp.float32)
            for (r, h), w in zip(pairs, weights)
        ]
        mixed = [
            o
            + (own[r, h] * v).astype(jnp.bfloat16).astype(jnp.float32) * new[r, h, :, HEAD_SIZE:]
            for (r, h), o, v in zip(pairs, mixed, inverse)
        ]
        mixed = jnp.stack(
            [
                jnp.concatenate(mixed[r * kv_heads : (r + 1) * kv_heads], axis=0)
                for r in range(ROWS_STEP)
            ],
            axis=0,
        )
        mixed = jnp.swapaxes(mixed, 0, 1)
        att[i] = jnp.concatenate([mixed[j] for j in range(q_heads)], axis=1)
        return carry

    lax.fori_loop(0, steps, attend, 0)
    load_gu.start()
    load_d.start()
    pl.semaphore_wait(barrier, bits + 1)
    load_o.wait()
    attended = att[...].reshape(halves * tokens, q_heads * HEAD_SIZE).astype(jnp.bfloat16)
    swaps = []
    for t in range(width // OUT_TILE):
        cols = slice(t * OUT_TILE, (t + 1) * OUT_TILE)
        y = jnp.dot(attended, wo[:, cols], preferred_element_type=jnp.float32)
        pout[t] = y.reshape(halves, tokens, OUT_TILE)
        swaps.append(remote(pout.at[t, 1 - g], xsib.at[t], xsend.at[t], xrecv.at[t], sib))
        swaps[-1].start()
    squares = jnp.zeros((tok, 1), jnp.float32)
    for t in range(width // OUT_TILE):
        cols = slice(t * OUT_TILE, (t + 1) * OUT_TILE)
        swaps[t].wait()
        h = res_ref[:, cols].astype(jnp.float32) + (pout[t, g] + xsib[t])
        hid[:, cols] = h
        squares = squares + jnp.sum(h * h, axis=-1, keepdims=True)
    inv_norm = lax.rsqrt(squares * (1.0 / width) + 1e-06)
    gain = gain_ref[...].astype(jnp.float32).reshape(1, width)
    normed = (hid[...] * inv_norm * gain).astype(jnp.bfloat16)
    logits = lax.dot_general(
        router_ref[...], normed, (((1,), (1,)), ((), ())), preferred_element_type=jnp.float32
    )
    name = lax.broadcasted_iota(jnp.int32, (experts, tok), 0)
    routes = routes_ref[...]
    routed = name == routes[0:1, :]
    for k in range(1, routes.shape[0]):
        routed = jnp.logical_or(routed, name == routes[k : k + 1, :])
    picked = jnp.where(routed, jnp.exp(logits), 0.0)
    gates = picked / jnp.sum(picked, axis=0, keepdims=True)
    extra = gath.shape[3] - width
    if extra > experts:
        gates = jnp.concatenate([gates, jnp.zeros((extra - experts, tok), jnp.float32)], axis=0)
    gates = jnp.concatenate([gates, jnp.zeros((extra, 128 - tok), jnp.float32)], axis=1)
    gath[0, 0, :, :width] = normed
    gath[0, 0, :, width:] = jnp.transpose(gates)[:tok].astype(jnp.bfloat16)

    sends = []

    def forward(slot):
        first = slot.bit_length()
        for j in range(first, bits):
            there = slot | (1 << j)
            sends.append(
                remote(gath.at[0, slot], gath.at[0, there], gsend.at[there], grecv.at[there], peers[j])
            )
            sends[-1].start()
        sends.append(remote(gath.at[0, slot], gath.at[1, slot], ssend.at[slot], srecv.at[slot], sib))
        sends[-1].start()

    def arrived(slot):
        remote(gath.at[0, slot], gath.at[0, slot], gsend.at[slot], grecv.at[slot], sib).wait_recv()

    def arrived_sib(slot):
        remote(gath.at[0, slot], gath.at[1, slot], ssend.at[slot], srecv.at[slot], sib).wait_recv()

    half = n // 2
    forward(0)
    for slot in range(1, half):
        arrived(slot)
        forward(slot)

    expert = g * n + d
    size = min(8, half)
    rows = 2 * size * tok

    def gate_up(base, t, tile):
        x = gath[:, pl.ds(base, size), :, :width].reshape(rows, width)
        gate = jnp.dot(x, wgu[:, t : t + tile], preferred_element_type=jnp.float32)
        up = jnp.dot(x, wgu[:, ff + t : ff + t + tile], preferred_element_type=jnp.float32)
        act[:, :, :, t : t + tile] = (
            (gate / (1.0 + jnp.exp(-gate)) * up).astype(jnp.bfloat16).reshape(2, size, tok, tile)
        )

    def down(base, start, count):
        span = slice(start, start + count)
        own_rows = 2 * count * tok
        weights = gath[:, base + start : base + start + count, :, width:]
        weights = weights.reshape(own_rows, extra).astype(jnp.float32)
        mine = lax.broadcasted_iota(jnp.int32, (own_rows, extra), 1) == expert
        weight = jnp.sum(jnp.where(mine, weights, 0.0), axis=1, keepdims=True)
        x = act[:, span].reshape(own_rows, ff)
        tile = 512
        for t in range(0, width, tile):
            y = jnp.dot(x, wd[:, t : t + tile], preferred_element_type=jnp.float32)
            y = (y * weight).astype(jnp.bfloat16).reshape(2, count, tok, tile)
            part[:, base + start : base + start + count, :, t : t + tile] = y

    FT = 256
    for slot in range(half):
        arrived_sib(slot)
    load_gu.wait()
    pending = list(range(half, n))
    tiles = list(range(0, ff, FT))
    for at in range(0, half, size):
        for t in tiles:
            gate_up(at, t, FT)
            if at == 0:
                count = -(-half // len(tiles))
                for slot in pending[:count]:
                    arrived(slot)
                    forward(slot)
                pending = pending[count:]
        if at == 0:
            load_d.wait()
        down(at, 0, size)

    def give(slot):
        sends.append(remote(part.at[1, slot], rsib.at[slot], bsend.at[slot], brecv.at[slot], sib))
        sends[-1].start()

    def add_to(slot, more):
        part[0, slot] = (part[0, slot].astype(jnp.float32) + more.astype(jnp.float32)).astype(
            jnp.bfloat16
        )

    def taken(slot):
        remote(part.at[1, slot], rsib.at[slot], bsend.at[slot], brecv.at[slot], sib).wait_recv()
        add_to(slot, rsib[slot])

    order = [bits - 2, bits - 1] + list(range(bits - 3, -1, -1)) if bits >= 2 else [0]
    first_bit = 1 << order[0]

    def ship(slot, step):
        sends.append(
            remote(
                part.at[0, slot],
                racc.at[slot],
                rsend.at[slot],
                rrecv.at[slot],
                peers[order[step]],
            )
        )
        sends[-1].start()

    def received(source):
        remote(part.at[0, 0], racc.at[source], rsend.at[source], rrecv.at[source], sib).wait_recv()

    def absorb(slot, step):
        source = slot | (1 << order[step])
        received(source)
        add_to(slot, racc[source])

    early = [s for s in range(half) if s & first_bit] + [s for s in range(half) if not s & first_bit]
    for slot in early:
        give(slot)
    for slot in range(half, n):
        arrived_sib(slot)
    waiting = list(early)
    for at in range(half, n, size):
        for t in tiles:
            gate_up(at, t, FT)
            if at == half:
                count = -(-half // len(tiles))
                for slot in waiting[:count]:
                    taken(slot)
                    if slot & first_bit:
                        ship(slot, 0)
                waiting = waiting[count:]
        cut = size // 2
        down(at, cut, size - cut)
        for slot in reversed(range(at + cut, at + size)):
            give(slot)
        down(at, 0, cut)
        for slot in reversed(range(at, at + cut)):
            give(slot)
    for slot in reversed(range(half, n)):
        taken(slot)
        if slot & first_bit:
            ship(slot, 0)

    live = [s for s in range(n) if not s & first_bit]
    for step in range(1, len(order)):
        out_going = [s for s in live if s & (1 << order[step])]
        staying = [s for s in live if not s & (1 << order[step])]
        for s in reversed(out_going):
            absorb(s, step - 1)
            ship(s, step)
        for s in reversed(staying):
            absorb(s, step - 1)
        live = staying
    source = 1 << order[-1]
    received(source)
    out_ref[...] = (
        hid[...] + (part[0, 0].astype(jnp.float32) + racc[source].astype(jnp.float32))
    ).astype(jnp.bfloat16)
    for copy in sends:
        copy.wait_send()


def layer(n, lens, queries, latest, cache, wo, residual, gain, router, routes, gate_up, down):
    tok, width = residual.shape
    bits = n.bit_length() - 1
    extra = -(-router.shape[0] // 128) * 128
    size = min(8, n // 2)
    halves, tokens, q_width = queries.shape
    per_half = tokens // ROWS_STEP
    tiles = width // OUT_TILE
    bf16, f32 = jnp.bfloat16, jnp.float32
    dma = pltpu.SemaphoreType.DMA
    vmem = pl.BlockSpec(memory_space=pltpu.VMEM)
    smem = pl.BlockSpec(memory_space=pltpu.SMEM)
    hbm = pl.BlockSpec(memory_space=pl.ANY)
    return pl.pallas_call(
        functools.partial(layer_kernel, n, bits),
        out_shape=jax.ShapeDtypeStruct((tok, width), bf16),
        in_specs=[smem, vmem, vmem, hbm, hbm, vmem, vmem, vmem, vmem, hbm, hbm],
        out_specs=vmem,
        scratch_shapes=[
            pltpu.VMEM((halves, per_half, ROWS_STEP) + cache.shape[2:], bf16),
            pltpu.VMEM(wo.shape, bf16),
            pltpu.VMEM(gate_up.shape[1:], bf16),
            pltpu.VMEM(down.shape[1:], bf16),
            pltpu.VMEM((halves, tokens, q_width // HEAD_SIZE, HEAD_SIZE), f32),
            pltpu.VMEM((halves * per_half, ROWS_STEP, q_width), f32),
            pltpu.VMEM((tiles, halves, tokens, OUT_TILE), f32),
            pltpu.VMEM((tiles, tok, OUT_TILE), f32),
            pltpu.VMEM((tok, width), f32),
            pltpu.VMEM((2, n, tok, width + extra), bf16),
            pltpu.VMEM((2, size, tok, down.shape[1]), bf16),
            pltpu.VMEM((2, n, tok, width), bf16),
            pltpu.VMEM((n, tok, width), bf16),
            pltpu.VMEM((n, tok, width), bf16),
            dma((halves, per_half)),
            dma((3,)),
            dma((tiles,)),
            dma((tiles,)),
        ]
        + [dma((n,))] * 8,
        compiler_params=pltpu.CompilerParams(
            collective_id=0, has_side_effects=True, vmem_limit_bytes=VMEM_LIMIT
        ),
        name="layer",
    )(lens, queries, latest, cache, wo, residual, gain, router, routes, gate_up, down)


def solution(mesh):
    n = mesh.shape["dev"]

    def per_device(
        residual_in,
        queries,
        latest_key_value,
        key_value_cache,
        cache_len,
        out_weight,
        norm_gain,
        router_weight,
        routes,
        expert_gate_up,
        expert_down,
    ):
        return layer(
            n,
            cache_len,
            queries,
            latest_key_value,
            key_value_cache,
            out_weight,
            residual_in,
            norm_gain,
            router_weight.T,
            routes.T,
            expert_gate_up,
            expert_down,
        )

    placed = (
        P(("grp", "dev"), None),
        P(None, "dev", "grp"),
        P(None, "dev", "grp", None),
        P(None, "dev", "grp", None, None),
        P(None, "dev"),
        P("grp", None),
        P(),
        P(),
        P(("grp", "dev"), None),
        P(("grp", "dev"), None, None),
        P(("grp", "dev"), None, None),
    )
    return jax.shard_map(
        per_device, mesh=mesh, in_specs=placed, out_specs=P(("grp", "dev"), None), check_vma=False
    )
```

time: 75.8 us -> 51.6 us (0.68)
  Pallas kernels: 69.2 us -> 49.9 us
  local copies, waits for them, and re-layouts: 6.35 us -> 1.47 us
    pallas_call x2 -> x1, Pallas kernels: 69.2 us -> 49.9 us  [layer(): pl.pallas_call(functools.partial(layer_kernel, n, bits), out_shape=jax.Sh...]
    reshape x2 -> x0, local copies, waits for them, and re-layouts: 2.53 us -> none  [the longest x1 1.29 us: per_device(): norm_gain.reshape(1, -1)]
    unnamed x5 -> x1, local copies, waits for them, and re-layouts: 3.82 us -> 1.47 us
where the time goes in v2:
time: 51.6 us; the launch traced here: 51.4 us
  Pallas kernels  49.9 us (97%)
  local copies, waits for them, and re-layouts  1.47 us (3%)
    pallas_call x1, Pallas kernels, layer(): pl.pallas_call(functools.partial(layer_kernel, n, bits), out_shape=jax.Sh...  49.9 us
    unnamed x1, local copies, waits for them, and re-layouts  1.47 us

profile of v2, /device:TPU:0, one launch (start us, length us, event | category | flops | bytes accessed | tf_op | source)
XLA Modules:
  0.0 51.4 jit_solution(11355030132057209660)
XLA Ops:
  0.0 49.9 %layer.1 = bf16[16,2048]{1,0:T(8,128)(2,1)} custom-call(s32[2,16]{1,0:T(2,128)} %lens_ref.1, bf16[2,16,2048]{2,1,0:T(8,128)(2,1)} %q_ref.1, bf16[2,16,2,256]{3,2,1,0:T(2,128)(2,1)} %new_ref.1, bf16[2,16,2,256,256]{4,3,2,1,0:T(8,128)(2,1)} %cache_hbm.1, bf16[2048,2048]{1,0:T(8,128)(2,1)} %wo_hbm.1, bf16[16,2048]{1,0:T(8,128)(2,1)} %res_ref.1, ...), custom_call_target="tpu_custom_call" | custom-call | tf_op jit(solution)/shard_map/layer/pallas_call | solution.py:376
  49.9 1.5 %copy.13 = bf16[16,2048]{1,0:T(8,128)(2,1)} copy(bf16[16,2048]{1,0:T(8,128)(2,1)} %layer.1) | data formatting | bytes 131072

commit v3 on v2

--- a/solution.py
+++ b/solution.py
@@ -13,6 +13,17 @@
 ROWS_STEP = 8
 OUT_TILE = 512
 VMEM_LIMIT = 60 * 1024 * 1024
+
+
+def plan(n, bits):
+    hops = [3.2 if j == 0 else 2.0 for j in range(bits)]
+
+    def due(slot):
+        return sum(hops[j] for j in range(bits) if slot & (1 << j))
+
+    slots = sorted(range(n), key=lambda slot: (due(slot), slot))
+    chunks = [n // 4, n // 2, n // 4] if n <= 16 else [8] * (n // 8)
+    return slots, chunks
 
 
 def layer_kernel(
@@ -208,95 +219,74 @@
     gath[0, 0, :, width:] = jnp.transpose(gates)[:tok].astype(jnp.bfloat16)
 
     sends = []
+    slots, chunks = plan(n, bits)
+    place_of = {slot: at for at, slot in enumerate(slots)}
+    order = [bits - 2, bits - 1] + list(range(bits - 3, -1, -1))
 
     def forward(slot):
-        first = slot.bit_length()
-        for j in range(first, bits):
+        at = place_of[slot]
+        for j in range(slot.bit_length(), bits):
             there = slot | (1 << j)
             sends.append(
-                remote(gath.at[0, slot], gath.at[0, there], gsend.at[there], grecv.at[there], peers[j])
+                remote(
+                    gath.at[0, at],
+                    gath.at[0, place_of[there]],
+                    gsend.at[there],
+                    grecv.at[there],
+                    peers[j],
+                )
             )
             sends[-1].start()
-        sends.append(remote(gath.at[0, slot], gath.at[1, slot], ssend.at[slot], srecv.at[slot], sib))
+        sends.append(remote(gath.at[0, at], gath.at[1, at], ssend.at[slot], srecv.at[slot], sib))
         sends[-1].start()
 
     def arrived(slot):
-        remote(gath.at[0, slot], gath.at[0, slot], gsend.at[slot], grecv.at[slot], sib).wait_recv()
+        at = gath.at[0, place_of[slot]]
+        remote(at, at, gsend.at[slot], grecv.at[slot], sib).wait_recv()
 
     def arrived_sib(slot):
-        remote(gath.at[0, slot], gath.at[1, slot], ssend.at[slot], srecv.at[slot], sib).wait_recv()
-
-    half = n // 2
+        at = place_of[slot]
+        remote(gath.at[0, at], gath.at[1, at], ssend.at[slot], srecv.at[slot], sib).wait_recv()
+
     forward(0)
-    for slot in range(1, half):
-        arrived(slot)
-        forward(slot)
-
     expert = g * n + d
-    size = min(8, half)
-    rows = 2 * size * tok
-
-    def gate_up(base, t, tile):
-        x = gath[:, pl.ds(base, size), :, :width].reshape(rows, width)
-        gate = jnp.dot(x, wgu[:, t : t + tile], preferred_element_type=jnp.float32)
-        up = jnp.dot(x, wgu[:, ff + t : ff + t + tile], preferred_element_type=jnp.float32)
-        act[:, :, :, t : t + tile] = (
-            (gate / (1.0 + jnp.exp(-gate)) * up).astype(jnp.bfloat16).reshape(2, size, tok, tile)
-        )
-
-    def down(base, start, count):
-        span = slice(start, start + count)
-        own_rows = 2 * count * tok
-        weights = gath[:, base + start : base + start + count, :, width:]
-        weights = weights.reshape(own_rows, extra).astype(jnp.float32)
-        mine = lax.broadcasted_iota(jnp.int32, (own_rows, extra), 1) == expert
-        weight = jnp.sum(jnp.where(mine, weights, 0.0), axis=1, keepdims=True)
-        x = act[:, span].reshape(own_rows, ff)
-        tile = 512
-        for t in range(0, width, tile):
-            y = jnp.dot(x, wd[:, t : t + tile], preferred_element_type=jnp.float32)
-            y = (y * weight).astype(jnp.bfloat16).reshape(2, count, tok, tile)
-            part[:, base + start : base + start + count, :, t : t + tile] = y
-
     FT = 256
-    for slot in range(half):
-        arrived_sib(slot)
-    load_gu.wait()
-    pending = list(range(half, n))
-    tiles = list(range(0, ff, FT))
-    for at in range(0, half, size):
-        for t in tiles:
-            gate_up(at, t, FT)
-            if at == 0:
-                count = -(-half // len(tiles))
-                for slot in pending[:count]:
-                    arrived(slot)
-                    forward(slot)
-                pending = pending[count:]
-        if at == 0:
-            load_d.wait()
-        down(at, 0, size)
+    DT = 512
+
+    def gate_up(start, count, t):
+        x = gath[:, start : start + count, :, :width].reshape(2 * count * tok, width)
+        gate = jnp.dot(x, wgu[:, t : t + FT], preferred_element_type=jnp.float32)
+        up = jnp.dot(x, wgu[:, ff + t : ff + t + FT], preferred_element_type=jnp.float32)
+        y = (gate / (1.0 + jnp.exp(-gate)) * up).astype(jnp.bfloat16)
+        act[:, :count, :, t : t + FT] = y.reshape(2, count, tok, FT)
+
+    def weigh(start, count):
+        weights = gath[:, start : start + count, :, width:]
+        weights = weights.reshape(2 * count * tok, extra).astype(jnp.float32)
+        mine = lax.broadcasted_iota(jnp.int32, weights.shape, 1) == expert
+        return jnp.sum(jnp.where(mine, weights, 0.0), axis=1, keepdims=True)
+
+    def down(start, count, t, weight):
+        x = act[:, :count].reshape(2 * count * tok, ff)
+        y = jnp.dot(x, wd[:, t : t + DT], preferred_element_type=jnp.float32)
+        y = (y * weight).astype(jnp.bfloat16).reshape(2, count, tok, DT)
+        part[:, start : start + count, :, t : t + DT] = y
 
     def give(slot):
-        sends.append(remote(part.at[1, slot], rsib.at[slot], bsend.at[slot], brecv.at[slot], sib))
+        at = place_of[slot]
+        sends.append(remote(part.at[1, at], rsib.at[slot], bsend.at[slot], brecv.at[slot], sib))
         sends[-1].start()
 
     def add_to(slot, more):
-        part[0, slot] = (part[0, slot].astype(jnp.float32) + more.astype(jnp.float32)).astype(
+        at = place_of[slot]
+        part[0, at] = (part[0, at].astype(jnp.float32) + more.astype(jnp.float32)).astype(
             jnp.bfloat16
         )
-
-    def taken(slot):
-        remote(part.at[1, slot], rsib.at[slot], bsend.at[slot], brecv.at[slot], sib).wait_recv()
-        add_to(slot, rsib[slot])
-
-    order = [bits - 2, bits - 1] + list(range(bits - 3, -1, -1)) if bits >= 2 else [0]
-    first_bit = 1 << order[0]
 
     def ship(slot, step):
         sends.append(
             remote(
-                part.at[0, slot],
+                part.at[0, place_of[slot]],
                 racc.at[slot],
                 rsend.at[slot],
                 rrecv.at[slot],
@@ -308,54 +298,76 @@
     def received(source):
         remote(part.at[0, 0], racc.at[source], rsend.at[source], rrecv.at[source], sib).wait_recv()
 
-    def absorb(slot, step):
-        source = slot | (1 << order[step])
-        received(source)
-        add_to(slot, racc[source])
-
-    early = [s for s in range(half) if s & first_bit] + [s for s in range(half) if not s & first_bit]
-    for slot in early:
-        give(slot)
-    for slot in range(half, n):
-        arrived_sib(slot)
-    waiting = list(early)
-    for at in range(half, n, size):
-        for t in tiles:
-            gate_up(at, t, FT)
-            if at == half:
-                count = -(-half // len(tiles))
-                for slot in waiting[:count]:
-                    taken(slot)
-                    if slot & first_bit:
-                        ship(slot, 0)
-                waiting = waiting[count:]
-        cut = size // 2
-        down(at, cut, size - cut)
-        for slot in reversed(range(at + cut, at + size)):
+    def taken(slot):
+        remote(part.at[1, 0], rsib.at[slot], bsend.at[slot], brecv.at[slot], sib).wait_recv()
+        add_to(slot, rsib[slot])
+        if slot & (1 << order[0]):
+            ship(slot, 0)
+
+    def step_of(slot):
+        return min(t for t in range(bits) if slot & (1 << order[t]))
+
+    def pump(slot):
+        arrived(slot)
+        forward(slot)
+
+    def spread(work, points):
+        share = -(-len(work) // points)
+        return [work[k * share : (k + 1) * share] for k in range(points)]
+
+    points = ff // FT + width // DT
+    start = 0
+    previous = []
+    for c, count in enumerate(chunks):
+        now = slots[start : start + count]
+        if c == 0:
+            for slot in now[1:]:
+                pump(slot)
+        for slot in now:
+            arrived_sib(slot)
+        if c == 0:
+            load_gu.wait()
+        ahead = slots[start + count : start + count + chunks[c + 1]] if c + 1 < len(chunks) else []
+        pumps = spread(ahead, points - 1) + [[]]
+        takes = spread(sorted(previous, key=lambda s: not s & (1 << order[0])), points - 1) + [[]]
+        k = 0
+        for t in range(0, ff, FT):
+            gate_up(start, count, t)
+            for slot in pumps[k]:
+                pump(slot)
+            for slot in takes[k]:
+                taken(slot)
+            k += 1
+        if c == 0:
+            load_d.wait()
+        weight = weigh(start, count)
+        for t in range(0, width, DT):
+            down(start, count, t, weight)
+            for slot in pumps[k]:
+                pump(slot)
+            for slot in takes[k]:
+                taken(slot)
+            k += 1
+        previous = sorted(now, key=lambda s: not s & (1 << order[0]))
+        for slot in previous:
             give(slot)
-        down(at, 0, cut)
-        for slot in reversed(range(at, at + cut)):
-            give(slot)
-    for slot in reversed(range(half, n)):
+        start += count
+    for slot in previous:
         taken(slot)
-        if slot & first_bit:
-            ship(slot, 0)
-
-    live = [s for s in range(n) if not s & first_bit]
-    for step in range(1, len(order)):
-        out_going = [s for s in live if s & (1 << order[step])]
-        staying = [s for s in live if not s & (1 << order[step])]
-        for s in reversed(out_going):
-            absorb(s, step - 1)
-            ship(s, step)
-        for s in reversed(staying):
-            absorb(s, step - 1)
-        live = staying
-    source = 1 << order[-1]
-    received(source)
-    out_ref[...] = (
-        hid[...] + (part[0, 0].astype(jnp.float32) + racc[source].astype(jnp.float32))
-    ).astype(jnp.bfloat16)
+
+    for step in range(1, bits):
+        for slot in slots[1:]:
+            if step_of(slot) == step:
+                for t in range(step):
+                    source = slot | (1 << order[t])
+                    received(source)
+                    add_to(slot, racc[source])
+                ship(slot, step)
+    total = hid[...] + part[0, 0].astype(jnp.float32)
+    for t in range(bits):
+        received(1 << order[t])
+        total = total + racc[1 << order[t]].astype(jnp.float32)
+    out_ref[...] = total
     for copy in sends:
         copy.wait_send()
 
@@ -364,7 +376,7 @@
     tok, width = residual.shape
     bits = n.bit_length() - 1
     extra = -(-router.shape[0] // 128) * 128
-    size = min(8, n // 2)
+    size = max(plan(n, bits)[1])
     halves, tokens, q_width = queries.shape
     per_half = tokens // ROWS_STEP
     tiles = width // OUT_TILE
@@ -375,7 +387,7 @@
     hbm = pl.BlockSpec(memory_space=pl.ANY)
     return pl.pallas_call(
         functools.partial(layer_kernel, n, bits),
-        out_shape=jax.ShapeDtypeStruct((tok, width), bf16),
+        out_shape=jax.ShapeDtypeStruct((tok, width), f32),
         in_specs=[smem, vmem, vmem, hbm, hbm, vmem, vmem, vmem, vmem, hbm, hbm],
         out_specs=vmem,
         scratch_shapes=[
@@ -435,7 +447,7 @@
             routes.T,
             expert_gate_up,
             expert_down,
-        )
+        ).astype(jnp.bfloat16)
 
     placed = (
         P(("grp", "dev"), None),

time: 51.6 us -> 56.4 us (1.093)
  Pallas kernels: 49.9 us -> 54.7 us
  other arithmetic: 0 us -> 1.54 us
  local copies, waits for them, and re-layouts: 1.47 us -> 0 us
    pallas_call x1, Pallas kernels: 49.9 us -> 54.7 us  [layer(): pl.pallas_call(functools.partial(layer_kernel, n, bits), out_shape=jax.Sh...]
    convert_element_type x0 -> x1, other arithmetic: none -> 1.54 us  [per_device(): return layer(n, cache_len, queries, latest_key_value, key_value_cache, ou...]
    unnamed x1 -> x0, local copies, waits for them, and re-layouts: 1.47 us -> none
where the time goes in v3:
time: 56.4 us; the launch traced here: 56.3 us
  Pallas kernels  54.7 us (97%)
  other arithmetic  1.54 us (3%)
    pallas_call x1, Pallas kernels, layer(): pl.pallas_call(functools.partial(layer_kernel, n, bits), out_shape=jax.Sh...  54.7 us
    convert_element_type x1, other arithmetic, per_device(): return layer(n, cache_len, queries, latest_key_value, key_value_cache, ou...  1.54 us

profile of v3, /device:TPU:0, one launch (start us, length us, event | category | flops | bytes accessed | tf_op | source)
XLA Modules:
  0.0 56.3 jit_solution(16440983121965639006)
XLA Ops:
  0.0 54.7 %layer.1 = f32[16,2048]{1,0:T(8,128)} custom-call(s32[2,16]{1,0:T(2,128)} %lens_ref.1, bf16[2,16,2048]{2,1,0:T(8,128)(2,1)} %q_ref.1, bf16[2,16,2,256]{3,2,1,0:T(2,128)(2,1)} %new_ref.1, bf16[2,16,2,256,256]{4,3,2,1,0:T(8,128)(2,1)} %cache_hbm.1, bf16[2048,2048]{1,0:T(8,128)(2,1)} %wo_hbm.1, bf16[16,2048]{1,0:T(8,128)(2,1)} %res_ref.1, ...), custom_call_target="tpu_custom_call" | custom-call | tf_op jit(solution)/shard_map/layer/pallas_call | solution.py:388
  54.7 1.5 %convert_element_type.3 = bf16[16,2048]{1,0:T(8,128)(2,1)} convert(f32[16,2048]{1,0:T(8,128)} %layer.1) | non-fusion elementwise | flops 32768 | bytes 196608 | tf_op jit(solution)/shard_map/convert_element_type | solution.py:450

commit v4 on v2

--- a/solution.py
+++ b/solution.py
@@ -12,6 +12,7 @@
 MESH = pl.DeviceIdType.MESH
 ROWS_STEP = 8
 OUT_TILE = 512
+FF_TILE = 256
 VMEM_LIMIT = 60 * 1024 * 1024
 
 
@@ -227,135 +228,157 @@
         remote(gath.at[0, slot], gath.at[1, slot], ssend.at[slot], srecv.at[slot], sib).wait_recv()
 
     half = n // 2
-    forward(0)
-    for slot in range(1, half):
-        arrived(slot)
-        forward(slot)
-
+    quarter = n // 4
     expert = g * n + d
     size = min(8, half)
     rows = 2 * size * tok
-
-    def gate_up(base, t, tile):
-        x = gath[:, pl.ds(base, size), :, :width].reshape(rows, width)
-        gate = jnp.dot(x, wgu[:, t : t + tile], preferred_element_type=jnp.float32)
-        up = jnp.dot(x, wgu[:, ff + t : ff + t + tile], preferred_element_type=jnp.float32)
-        act[:, :, :, t : t + tile] = (
-            (gate / (1.0 + jnp.exp(-gate)) * up).astype(jnp.bfloat16).reshape(2, size, tok, tile)
-        )
-
-    def down(base, start, count):
-        span = slice(start, start + count)
-        own_rows = 2 * count * tok
-        weights = gath[:, base + start : base + start + count, :, width:]
-        weights = weights.reshape(own_rows, extra).astype(jnp.float32)
-        mine = lax.broadcasted_iota(jnp.int32, (own_rows, extra), 1) == expert
-        weight = jnp.sum(jnp.where(mine, weights, 0.0), axis=1, keepdims=True)
-        x = act[:, span].reshape(own_rows, ff)
-        tile = 512
-        for t in range(0, width, tile):
-            y = jnp.dot(x, wd[:, t : t + tile], preferred_element_type=jnp.float32)
-            y = (y * weight).astype(jnp.bfloat16).reshape(2, count, tok, tile)
-            part[:, base + start : base + start + count, :, t : t + tile] = y
-
-    FT = 256
+    tiles = width // OUT_TILE
+
+    def due(slot):
+        return sum((3 if j == 0 else 2) for j in range(bits) if slot & (1 << j))
+
+    forward(0)
+    for slot in sorted(range(1, half), key=due):
+        arrived(slot)
+        forward(slot)
+
+    def gate_up(base, t):
+        x = gath[:, base : base + size, :, :width].reshape(rows, width)
+        gate = jnp.dot(x, wgu[:, t : t + FF_TILE], preferred_element_type=jnp.float32)
+        up = jnp.dot(x, wgu[:, ff + t : ff + t + FF_TILE], preferred_element_type=jnp.float32)
+        act[:, t : t + FF_TILE] = (gate / (1.0 + jnp.exp(-gate)) * up).astype(jnp.bfloat16)
+
+    def weigh(base):
+        weights = gath[:, base : base + size, :, width:].reshape(rows, extra).astype(jnp.float32)
+        mine = lax.broadcasted_iota(jnp.int32, (rows, extra), 1) == expert
+        return jnp.sum(jnp.where(mine, weights, 0.0), axis=1, keepdims=True)
+
+    def down(base, t, weight):
+        y = jnp.dot(
+            act[...], wd[:, t * OUT_TILE : (t + 1) * OUT_TILE], preferred_element_type=jnp.float32
+        )
+        part[t, :, base : base + size] = (
+            (y * weight).astype(jnp.bfloat16).reshape(2, size, tok, OUT_TILE)
+        )
+
+    def give(t, which):
+        span = pl.ds(which * half, half)
+        sends.append(
+            remote(
+                part.at[t, 1, span], rsib.at[t, span], bsend.at[t, which], brecv.at[t, which], sib
+            )
+        )
+        sends[-1].start()
+
+    def add_to(t, low, high, more):
+        part[t, 0, low:high] = (
+            part[t, 0, low:high].astype(jnp.float32) + more.astype(jnp.float32)
+        ).astype(jnp.bfloat16)
+
+    def hop(t, low, count, index, j):
+        span = pl.ds(low, count)
+        return remote(
+            part.at[t, 0, span], racc.at[t, span], rsend.at[t, index], rrecv.at[t, index], peers[j]
+        )
+
+    def ship(*where):
+        sends.append(hop(*where))
+        sends[-1].start()
+
+    def take(t, which):
+        span = pl.ds(which * half, half)
+        remote(
+            part.at[t, 1, span], rsib.at[t, span], bsend.at[t, which], brecv.at[t, which], sib
+        ).wait_recv()
+        low = which * half
+        far = low + quarter
+        add_to(t, far, far + quarter, rsib[t, far : far + quarter])
+        ship(t, far, quarter, which, bits - 2)
+        add_to(t, low, far, rsib[t, low:far])
+
+    def second(t):
+        hop(t, half + quarter, quarter, 1, bits - 2).wait_recv()
+        add_to(t, half, half + quarter, racc[t, half + quarter : n])
+        ship(t, half, quarter, 2, bits - 1)
+
+    def third(t):
+        hop(t, quarter, quarter, 0, bits - 2).wait_recv()
+        add_to(t, 0, quarter, racc[t, quarter:half])
+        hop(t, half, quarter, 2, bits - 1).wait_recv()
+        add_to(t, 0, quarter, racc[t, half : half + quarter])
+        if bits > 2:
+            m = quarter // 2
+            ship(t, m, m, 3, bits - 3)
+
+    def later(t, k):
+        m = quarter >> (k + 1)
+        hop(t, m, m, 3 + k, bits - 3 - k).wait_recv()
+        add_to(t, 0, m, racc[t, m : 2 * m])
+        ship(t, m // 2, m // 2, 4 + k, bits - 4 - k)
+
+    def last(t):
+        cols = slice(t * OUT_TILE, (t + 1) * OUT_TILE)
+        total = hid[:, cols] + part[t, 0, 0].astype(jnp.float32)
+        if bits > 2:
+            hop(t, 1, 1, bits, 0).wait_recv()
+            total = total + racc[t, 1].astype(jnp.float32)
+        out_ref[:, cols] = total.astype(jnp.bfloat16)
+
     for slot in range(half):
         arrived_sib(slot)
     load_gu.wait()
-    pending = list(range(half, n))
-    tiles = list(range(0, ff, FT))
+    pending = sorted(range(half, n), key=due)
+    share = -(-half // 4)
     for at in range(0, half, size):
-        for t in tiles:
-            gate_up(at, t, FT)
+        for t in range(0, ff, FF_TILE):
+            gate_up(at, t)
             if at == 0:
-                count = -(-half // len(tiles))
-                for slot in pending[:count]:
+                for slot in pending[:share]:
                     arrived(slot)
                     forward(slot)
-                pending = pending[count:]
+                pending = pending[share:]
         if at == 0:
             load_d.wait()
-        down(at, 0, size)
-
-    def give(slot):
-        sends.append(remote(part.at[1, slot], rsib.at[slot], bsend.at[slot], brecv.at[slot], sib))
-        sends[-1].start()
-
-    def add_to(slot, more):
-        part[0, slot] = (part[0, slot].astype(jnp.float32) + more.astype(jnp.float32)).astype(
-            jnp.bfloat16
-        )
-
-    def taken(slot):
-        remote(part.at[1, slot], rsib.at[slot], bsend.at[slot], brecv.at[slot], sib).wait_recv()
-        add_to(slot, rsib[slot])
-
-    order = [bits - 2, bits - 1] + list(range(bits - 3, -1, -1)) if bits >= 2 else [0]
-    first_bit = 1 << order[0]
-
-    def ship(slot, step):
-        sends.append(
-            remote(
-                part.at[0, slot],
-                racc.at[slot],
-                rsend.at[slot],
-                rrecv.at[slot],
-                peers[order[step]],
-            )
-        )
-        sends[-1].start()
-
-    def received(source):
-        remote(part.at[0, 0], racc.at[source], rsend.at[source], rrecv.at[source], sib).wait_recv()
-
-    def absorb(slot, step):
-        source = slot | (1 << order[step])
-        received(source)
-        add_to(slot, racc[source])
-
-    early = [s for s in range(half) if s & first_bit] + [s for s in range(half) if not s & first_bit]
-    for slot in early:
-        give(slot)
+        weight = weigh(at)
+        for t in range(tiles):
+            down(at, t, weight)
+            if at + size == half:
+                give(t, 0)
+            if at == 0:
+                for slot in pending[:share]:
+                    arrived(slot)
+                    forward(slot)
+                pending = pending[share:]
+    for slot in pending:
+        arrived(slot)
+        forward(slot)
     for slot in range(half, n):
         arrived_sib(slot)
-    waiting = list(early)
+    waiting = list(range(tiles))
     for at in range(half, n, size):
-        for t in tiles:
-            gate_up(at, t, FT)
-            if at == half:
-                count = -(-half // len(tiles))
-                for slot in waiting[:count]:
-                    taken(slot)
-                    if slot & first_bit:
-                        ship(slot, 0)
-                waiting = waiting[count:]
-        cut = size // 2
-        down(at, cut, size - cut)
-        for slot in reversed(range(at + cut, at + size)):
-            give(slot)
-        down(at, 0, cut)
-        for slot in reversed(range(at, at + cut)):
-            give(slot)
-    for slot in reversed(range(half, n)):
-        taken(slot)
-        if slot & first_bit:
-            ship(slot, 0)
-
-    live = [s for s in range(n) if not s & first_bit]
-    for step in range(1, len(order)):
-        out_going = [s for s in live if s & (1 << order[step])]
-        staying = [s for s in live if not s & (1 << order[step])]
-        for s in reversed(out_going):
-            absorb(s, step - 1)
-            ship(s, step)
-        for s in reversed(staying):
-            absorb(s, step - 1)
-        live = staying
-    source = 1 << order[-1]
-    received(source)
-    out_ref[...] = (
-        hid[...] + (part[0, 0].astype(jnp.float32) + racc[source].astype(jnp.float32))
-    ).astype(jnp.bfloat16)
+        for t in range(0, ff, FF_TILE):
+            gate_up(at, t)
+            for k in waiting[:2]:
+                take(k, 0)
+            waiting = waiting[2:]
+        weight = weigh(at)
+        for t in range(tiles):
+            down(at, t, weight)
+            if at + size == n:
+                give(t, 1)
+                if t >= 2:
+                    take(t - 2, 1)
+    for k in waiting:
+        take(k, 0)
+    stages = [second, third] + [functools.partial(later, k=k) for k in range(bits - 3)] + [last]
+    for t in range(tiles - 2, tiles):
+        take(t, 1)
+        second(t - 2)
+    for turn in range(1, tiles + len(stages)):
+        for k in range(len(stages)):
+            t = turn - k
+            if 0 <= t < tiles and not (k == 0 and t < 2):
+                stages[k](t)
     for copy in sends:
         copy.wait_send()
 
@@ -389,16 +412,23 @@
             pltpu.VMEM((tiles, tok, OUT_TILE), f32),
             pltpu.VMEM((tok, width), f32),
             pltpu.VMEM((2, n, tok, width + extra), bf16),
-            pltpu.VMEM((2, size, tok, down.shape[1]), bf16),
-            pltpu.VMEM((2, n, tok, width), bf16),
-            pltpu.VMEM((n, tok, width), bf16),
-            pltpu.VMEM((n, tok, width), bf16),
+            pltpu.VMEM((2 * size * tok, down.shape[1]), bf16),
+            pltpu.VMEM((tiles, 2, n, tok, OUT_TILE), bf16),
+            pltpu.VMEM((tiles, n, tok, OUT_TILE), bf16),
+            pltpu.VMEM((tiles, n, tok, OUT_TILE), bf16),
             dma((halves, per_half)),
             dma((3,)),
             dma((tiles,)),
             dma((tiles,)),
-        ]
-        + [dma((n,))] * 8,
+            dma((n,)),
+            dma((n,)),
+            dma((n,)),
+            dma((n,)),
+            dma((tiles, 2)),
+            dma((tiles, 2)),
+            dma((tiles, bits + 1)),
+            dma((tiles, bits + 1)),
+        ],
         compiler_params=pltpu.CompilerParams(
             collective_id=0, has_side_effects=True, vmem_limit_bytes=VMEM_LIMIT
         ),

time: 51.6 us -> 58.6 us (1.14)
  Pallas kernels: 49.9 us -> 56.9 us
    pallas_call x1, Pallas kernels: 49.9 us -> 56.9 us  [layer(): pl.pallas_call(functools.partial(layer_kernel, n, bits), out_shape=jax.Sh...]
where the time goes in v4:
time: 58.6 us; the launch traced here: 58.4 us
  Pallas kernels  56.9 us (97%)
  local copies, waits for them, and re-layouts  1.47 us (3%)
    pallas_call x1, Pallas kernels, layer(): pl.pallas_call(functools.partial(layer_kernel, n, bits), out_shape=jax.Sh...  56.9 us
    unnamed x1, local copies, waits for them, and re-layouts  1.47 us

profile of v4, /device:TPU:0, one launch (start us, length us, event | category | flops | bytes accessed | tf_op | source)
XLA Modules:
  0.0 58.4 jit_solution(724748580033357849)
XLA Ops:
  0.0 56.9 %layer.1 = bf16[16,2048]{1,0:T(8,128)(2,1)} custom-call(s32[2,16]{1,0:T(2,128)} %lens_ref.1, bf16[2,16,2048]{2,1,0:T(8,128)(2,1)} %q_ref.1, bf16[2,16,2,256]{3,2,1,0:T(2,128)(2,1)} %new_ref.1, bf16[2,16,2,256,256]{4,3,2,1,0:T(8,128)(2,1)} %cache_hbm.1, bf16[2048,2048]{1,0:T(8,128)(2,1)} %wo_hbm.1, bf16[16,2048]{1,0:T(8,128)(2,1)} %res_ref.1, ...), custom_call_target="tpu_custom_call" | custom-call | tf_op jit(solution)/shard_map/layer/pallas_call | solution.py:399
  56.9 1.5 %copy.13 = bf16[16,2048]{1,0:T(8,128)(2,1)} copy(bf16[16,2048]{1,0:T(8,128)(2,1)} %layer.1) | data formatting | bytes 131072

commit v5 on v2

--- a/solution.py
+++ b/solution.py
@@ -173,26 +173,98 @@
     pl.semaphore_wait(barrier, bits + 1)
     load_o.wait()
     attended = att[...].reshape(halves * tokens, q_heads * HEAD_SIZE).astype(jnp.bfloat16)
+    sends = []
+    parts = len(gath)
+
+    def forward(c, slot):
+        for j in range(slot.bit_length(), bits):
+            there = slot | (1 << j)
+            sends.append(
+                remote(
+                    gath[c].at[0, slot],
+                    gath[c].at[0, there],
+                    gsend.at[c, there],
+                    grecv.at[c, there],
+                    peers[j],
+                )
+            )
+            sends[-1].start()
+        sends.append(
+            remote(
+                gath[c].at[0, slot],
+                gath[c].at[1, slot],
+                ssend.at[c, slot],
+                srecv.at[c, slot],
+                sib,
+            )
+        )
+        sends[-1].start()
+
+    def pump(c, slot):
+        at = gath[c].at[0, slot]
+        remote(at, at, gsend.at[c, slot], grecv.at[c, slot], sib).wait_recv()
+        forward(c, slot)
+
+    def arrived_sib(slot):
+        for c in range(parts):
+            remote(
+                gath[c].at[0, slot],
+                gath[c].at[1, slot],
+                ssend.at[c, slot],
+                srecv.at[c, slot],
+                sib,
+            ).wait_recv()
+
+    tiles = width // OUT_TILE
+    per_part = tiles // parts
+    wide = width // parts
+    extra = gath[-1].shape[3] - wide
     swaps = []
-    for t in range(width // OUT_TILE):
-        cols = slice(t * OUT_TILE, (t + 1) * OUT_TILE)
-        y = jnp.dot(attended, wo[:, cols], preferred_element_type=jnp.float32)
+
+    def project(t):
+        y = jnp.dot(
+            attended, wo[:, t * OUT_TILE : (t + 1) * OUT_TILE], preferred_element_type=jnp.float32
+        )
         pout[t] = y.reshape(halves, tokens, OUT_TILE)
         swaps.append(remote(pout.at[t, 1 - g], xsib.at[t], xsend.at[t], xrecv.at[t], sib))
         swaps[-1].start()
-    squares = jnp.zeros((tok, 1), jnp.float32)
-    for t in range(width // OUT_TILE):
-        cols = slice(t * OUT_TILE, (t + 1) * OUT_TILE)
-        swaps[t].wait()
-        h = res_ref[:, cols].astype(jnp.float32) + (pout[t, g] + xsib[t])
-        hid[:, cols] = h
-        squares = squares + jnp.sum(h * h, axis=-1, keepdims=True)
-    inv_norm = lax.rsqrt(squares * (1.0 / width) + 1e-06)
-    gain = gain_ref[...].astype(jnp.float32).reshape(1, width)
-    normed = (hid[...] * inv_norm * gain).astype(jnp.bfloat16)
-    logits = lax.dot_general(
-        router_ref[...], normed, (((1,), (1,)), ((), ())), preferred_element_type=jnp.float32
-    )
+
+    def settle(c):
+        squares = jnp.zeros((tok, 1), jnp.float32)
+        for t in range(c * per_part, (c + 1) * per_part):
+            cols = slice(t * OUT_TILE, (t + 1) * OUT_TILE)
+            swaps[t].wait()
+            h = res_ref[:, cols].astype(jnp.float32) + (pout[t, g] + xsib[t])
+            hid[:, cols] = h
+            squares = squares + jnp.sum(h * h, axis=-1, keepdims=True)
+        cols = slice(c * wide, (c + 1) * wide)
+        gain = gain_ref[...].astype(jnp.float32).reshape(1, width)[:, cols]
+        scaled = (hid[:, cols] * gain).astype(jnp.bfloat16)
+        gath[c][0, 0, :, :wide] = scaled
+        return squares, scaled
+
+    def partial_logits(c, scaled):
+        return lax.dot_general(
+            router_ref[:, c * wide : (c + 1) * wide],
+            scaled,
+            (((1,), (1,)), ((), ())),
+            preferred_element_type=jnp.float32,
+        )
+
+    for t in range(per_part + 1):
+        project(t)
+    squares, scaled = settle(0)
+    forward(0, 0)
+    logits = partial_logits(0, scaled)
+    for t in range(per_part + 1, tiles):
+        project(t)
+    more, scaled = settle(1)
+    logits = logits + partial_logits(1, scaled)
+    inv_norm = lax.rsqrt((squares + more) * (1.0 / width) + 1e-06)
+    square = jnp.broadcast_to(inv_norm, (tok, 128))
+    square = jnp.concatenate([square, jnp.zeros((128 - tok, 128), jnp.float32)], axis=0)
+    inv_row = jnp.transpose(square)[0:1, :tok]
+    logits = logits * inv_row
     name = lax.broadcasted_iota(jnp.int32, (experts, tok), 0)
     routes = routes_ref[...]
     routed = name == routes[0:1, :]
@@ -200,58 +272,56 @@
         routed = jnp.logical_or(routed, name == routes[k : k + 1, :])
     picked = jnp.where(routed, jnp.exp(logits), 0.0)
     gates = picked / jnp.sum(picked, axis=0, keepdims=True)
-    extra = gath.shape[3] - width
     if extra > experts:
         gates = jnp.concatenate([gates, jnp.zeros((extra - experts, tok), jnp.float32)], axis=0)
     gates = jnp.concatenate([gates, jnp.zeros((extra, 128 - tok), jnp.float32)], axis=1)
-    gath[0, 0, :, :width] = normed
-    gath[0, 0, :, width:] = jnp.transpose(gates)[:tok].astype(jnp.bfloat16)
-
-    sends = []
-
-    def forward(slot):
-        first = slot.bit_length()
-        for j in range(first, bits):
-            there = slot | (1 << j)
-            sends.append(
-                remote(gath.at[0, slot], gath.at[0, there], gsend.at[there], grecv.at[there], peers[j])
-            )
-            sends[-1].start()
-        sends.append(remote(gath.at[0, slot], gath.at[1, slot], ssend.at[slot], srecv.at[slot], sib))
-        sends[-1].start()
-
-    def arrived(slot):
-        remote(gath.at[0, slot], gath.at[0, slot], gsend.at[slot], grecv.at[slot], sib).wait_recv()
-
-    def arrived_sib(slot):
-        remote(gath.at[0, slot], gath.at[1, slot], ssend.at[slot], srecv.at[slot], sib).wait_recv()
+    gates = jnp.transpose(gates)[:tok]
+    lane = lax.broadcasted_iota(jnp.int32, (tok, extra), 1)
+    high = inv_norm.astype(jnp.bfloat16).astype(jnp.float32)
+    gates = jnp.where(lane == extra - 2, high, gates)
+    gates = jnp.where(lane == extra - 1, inv_norm - high, gates)
+    gath[1][0, 0, :, wide:] = gates.astype(jnp.bfloat16)
+    forward(1, 0)
 
     half = n // 2
-    forward(0)
-    for slot in range(1, half):
-        arrived(slot)
-        forward(slot)
+    early = list(range(1, half))
+    lead = min(3, len(early))
+    for slot in early[:lead]:
+        pump(0, slot)
+    for k, slot in enumerate(early):
+        if k + lead < len(early):
+            pump(0, early[k + lead])
+        pump(1, slot)
 
     expert = g * n + d
     size = min(8, half)
     rows = 2 * size * tok
 
+    def notes(base, start, count):
+        own = gath[1][:, base + start : base + start + count, :, wide:]
+        own = own.reshape(2 * count * tok, extra).astype(jnp.float32)
+        return own, lax.broadcasted_iota(jnp.int32, own.shape, 1)
+
     def gate_up(base, t, tile):
-        x = gath[:, pl.ds(base, size), :, :width].reshape(rows, width)
-        gate = jnp.dot(x, wgu[:, t : t + tile], preferred_element_type=jnp.float32)
-        up = jnp.dot(x, wgu[:, ff + t : ff + t + tile], preferred_element_type=jnp.float32)
+        own, lane = notes(base, 0, size)
+        norm = jnp.sum(jnp.where(lane >= extra - 2, own, 0.0), axis=1, keepdims=True)
+        x = jnp.concatenate(
+            [
+                gath[c][:, base : base + size, :, :wide].reshape(rows, wide)
+                for c in range(parts)
+            ],
+            axis=1,
+        )
+        gate = norm * jnp.dot(x, wgu[:, t : t + tile], preferred_element_type=jnp.float32)
+        up = norm * jnp.dot(x, wgu[:, ff + t : ff + t + tile], preferred_element_type=jnp.float32)
         act[:, :, :, t : t + tile] = (
             (gate / (1.0 + jnp.exp(-gate)) * up).astype(jnp.bfloat16).reshape(2, size, tok, tile)
         )
 
     def down(base, start, count):
-        span = slice(start, start + count)
-        own_rows = 2 * count * tok
-        weights = gath[:, base + start : base + start + count, :, width:]
-        weights = weights.reshape(own_rows, extra).astype(jnp.float32)
-        mine = lax.broadcasted_iota(jnp.int32, (own_rows, extra), 1) == expert
-        weight = jnp.sum(jnp.where(mine, weights, 0.0), axis=1, keepdims=True)
-        x = act[:, span].reshape(own_rows, ff)
+        own, lane = notes(base, start, count)
+        weight = jnp.sum(jnp.where(lane == expert, own, 0.0), axis=1, keepdims=True)
+        x = act[:, start : start + count].reshape(2 * count * tok, ff)
         tile = 512
         for t in range(0, width, tile):
             y = jnp.dot(x, wd[:, t : t + tile], preferred_element_type=jnp.float32)
@@ -262,17 +332,20 @@
     for slot in range(half):
         arrived_sib(slot)
     load_gu.wait()
-    pending = list(range(half, n))
+    quarter = half // 2
+    pending = []
+    for low in (half, half + quarter):
+        for c in range(parts):
+            pending += [(c, slot) for slot in range(low, low + quarter)]
     tiles = list(range(0, ff, FT))
+    share = -(-len(pending) // len(tiles))
     for at in range(0, half, size):
         for t in tiles:
             gate_up(at, t, FT)
             if at == 0:
-                count = -(-half // len(tiles))
-                for slot in pending[:count]:
-                    arrived(slot)
-                    forward(slot)
-                pending = pending[count:]
+                for c, slot in pending[:share]:
+                    pump(c, slot)
+                pending = pending[share:]
         if at == 0:
             load_d.wait()
         down(at, 0, size)
@@ -363,7 +436,7 @@
 def layer(n, lens, queries, latest, cache, wo, residual, gain, router, routes, gate_up, down):
     tok, width = residual.shape
     bits = n.bit_length() - 1
-    extra = -(-router.shape[0] // 128) * 128
+    extra = -(-(router.shape[0] + 2) // 128) * 128
     size = min(8, n // 2)
     halves, tokens, q_width = queries.shape
     per_half = tokens // ROWS_STEP
@@ -388,7 +461,10 @@
             pltpu.VMEM((tiles, halves, tokens, OUT_TILE), f32),
             pltpu.VMEM((tiles, tok, OUT_TILE), f32),
             pltpu.VMEM((tok, width), f32),
-            pltpu.VMEM((2, n, tok, width + extra), bf16),
+            [
+                pltpu.VMEM((2, n, tok, width // 2), bf16),
+                pltpu.VMEM((2, n, tok, width // 2 + extra), bf16),
+            ],
             pltpu.VMEM((2, size, tok, down.shape[1]), bf16),
             pltpu.VMEM((2, n, tok, width), bf16),
             pltpu.VMEM((n, tok, width), bf16),
@@ -398,7 +474,8 @@
             dma((tiles,)),
             dma((tiles,)),
         ]
-        + [dma((n,))] * 8,
+        + [dma((2, n))] * 4
+        + [dma((n,))] * 4,
         compiler_params=pltpu.CompilerParams(
             collective_id=0, has_side_effects=True, vmem_limit_bytes=VMEM_LIMIT
         ),

time: 51.6 us -> 52.2 us (1.012)
  Pallas kernels: 49.9 us -> 50.5 us
    pallas_call x1, Pallas kernels: 49.9 us -> 50.5 us  [layer(): pl.pallas_call(functools.partial(layer_kernel, n, bits), out_shape=jax.Sh...]
where the time goes in v5:
time: 52.2 us; the launch traced here: 52 us
  Pallas kernels  50.5 us (97%)
  local copies, waits for them, and re-layouts  1.47 us (3%)
    pallas_call x1, Pallas kernels, layer(): pl.pallas_call(functools.partial(layer_kernel, n, bits), out_shape=jax.Sh...  50.5 us
    unnamed x1, local copies, waits for them, and re-layouts  1.47 us

profile of v5, /device:TPU:0, one launch (start us, length us, event | category | flops | bytes accessed | tf_op | source)
XLA Modules:
  0.0 52.0 jit_solution(12141434330154498182)
XLA Ops:
  0.0 50.5 %layer.1 = bf16[16,2048]{1,0:T(8,128)(2,1)} custom-call(s32[2,16]{1,0:T(2,128)} %lens_ref.1, bf16[2,16,2048]{2,1,0:T(8,128)(2,1)} %q_ref.1, bf16[2,16,2,256]{3,2,1,0:T(2,128)(2,1)} %new_ref.1, bf16[2,16,2,256,256]{4,3,2,1,0:T(8,128)(2,1)} %cache_hbm.1, bf16[2048,2048]{1,0:T(8,128)(2,1)} %wo_hbm.1, bf16[16,2048]{1,0:T(8,128)(2,1)} %res_ref.1, ...), custom_call_target="tpu_custom_call" | custom-call | tf_op jit(solution)/shard_map/layer/pallas_call | solution.py:449
  50.5 1.5 %copy.13 = bf16[16,2048]{1,0:T(8,128)(2,1)} copy(bf16[16,2048]{1,0:T(8,128)(2,1)} %layer.1) | data formatting | bytes 131072

commit v6 on v2

--- a/solution.py
+++ b/solution.py
@@ -329,12 +329,8 @@
                     if slot & first_bit:
                         ship(slot, 0)
                 waiting = waiting[count:]
-        cut = size // 2
-        down(at, cut, size - cut)
-        for slot in reversed(range(at + cut, at + size)):
-            give(slot)
-        down(at, 0, cut)
-        for slot in reversed(range(at, at + cut)):
+        down(at, 0, size)
+        for slot in reversed(range(at, at + size)):
             give(slot)
     for slot in reversed(range(half, n)):
         taken(slot)

time: 51.6 us -> 52 us (level)
  no operation moved by 1% of the time
where the time goes in v6:
time: 52 us; the launch traced here: 51.8 us
  Pallas kernels  50.3 us (97%)
  local copies, waits for them, and re-layouts  1.47 us (3%)
    pallas_call x1, Pallas kernels, layer(): pl.pallas_call(functools.partial(layer_kernel, n, bits), out_shape=jax.Sh...  50.3 us
    unnamed x1, local copies, waits for them, and re-layouts  1.47 us

profile of v6, /device:TPU:0, one launch (start us, length us, event | category | flops | bytes accessed | tf_op | source)
XLA Modules:
  0.0 51.8 jit_solution(4704944717058962880)
XLA Ops:
  0.0 50.3 %layer.1 = bf16[16,2048]{1,0:T(8,128)(2,1)} custom-call(s32[2,16]{1,0:T(2,128)} %lens_ref.1, bf16[2,16,2048]{2,1,0:T(8,128)(2,1)} %q_ref.1, bf16[2,16,2,256]{3,2,1,0:T(2,128)(2,1)} %new_ref.1, bf16[2,16,2,256,256]{4,3,2,1,0:T(8,128)(2,1)} %cache_hbm.1, bf16[2048,2048]{1,0:T(8,128)(2,1)} %wo_hbm.1, bf16[16,2048]{1,0:T(8,128)(2,1)} %res_ref.1, ...), custom_call_target="tpu_custom_call" | custom-call | tf_op jit(solution)/shard_map/layer/pallas_call | solution.py:372
  50.3 1.5 %copy.13 = bf16[16,2048]{1,0:T(8,128)(2,1)} copy(bf16[16,2048]{1,0:T(8,128)(2,1)} %layer.1) | data formatting | bytes 131072
